TPU v7x, 32 devices: a whole 2x2x4 slice. The times are simulated.
32 devices in a mesh: ctx: 4 (over y, core), head: 2 (over x), seq: 4 (over z).
Axes of the slice: x: 2, y: 2, z: 4, core: 2. Of those that a mesh axis runs over, the one named last changes fastest.
Arguments:
- queries: bfloat16 [2048, 64, 128], P(('seq', 'ctx'), 'head'), parts along dimension 0, may hold values from -100 to 100
- keys: bfloat16 [2048, 4, 128], P(('seq', 'ctx'), 'head'), parts along dimension 0, may hold values from -8 to 8
- values: bfloat16 [2048, 4, 128], P(('seq', 'ctx'), 'head'), parts along dimension 0, may hold values from -6 to 6
Outputs:
- attended: bfloat16 [2048, 64, 128], P(('seq', 'ctx'), 'head'), parts along dimension 0
There are 4 independent parts, one for each index of `seq`. A program takes and returns all parts, laid end to end along the dimension named above; each array names one. Nothing has to cross between parts.
All inputs are finite; a program needn't handle non-finite values.
Results may differ from a plain program's by a relative error of at most 0.0035.
Values may be sent and summed in bfloat16 or wider, within the bound.
No kernel may reach another device: no remote copies, remote signals or barrier semaphores. Data moves between devices by JAX's collectives and lax.ppermute only.
A program may use at most 64 MiB of HBM per device.

v0:
```python
import math

import jax
import jax.numpy as jnp
from jax import lax
from jax.sharding import PartitionSpec as P


def local(queries, keys, values):
    row_count = queries.shape[0]
    dev_index = lax.axis_index("ctx")
    kv_heads = keys.shape[1]
    group_size = queries.shape[1] // kv_heads
    head_width = queries.shape[2]
    scale = 1.0 / math.sqrt(head_width)
    local_rows = jnp.arange(row_count, dtype=jnp.int32)
    query_places = dev_index * row_count + local_rows
    tile_rows = math.gcd(row_count, 16)
    tile_count = row_count // tile_rows
    grouped = queries.reshape(tile_count, tile_rows, kv_heads, group_size, head_width)
    tile_places = query_places.reshape(tile_count, tile_rows)
    tile_last = jnp.max(tile_places, axis=1)

    def absorb(state_now, query_tile, places_tile, key_block, value_block, key_places):
        top_old, total_old, numerator = state_now
        scores = (
            jnp.einsum("rkgd,nkd->rkgn", query_tile, key_block, preferred_element_type=jnp.float32)
            * scale
        )
        visible = key_places[None, None, None, :] <= places_tile[:, None, None, None]
        scores = jnp.where(visible, scores, -1e30)
        top_new = jnp.maximum(top_old, jnp.max(scores, axis=-1))
        weights = jnp.where(visible, jnp.exp(scores - top_new[..., None]), 0.0)
        rescale = jnp.exp(top_old - top_new)
        total_new = total_old * rescale + jnp.sum(weights, axis=-1)
        numerator = numerator * rescale[..., None] + jnp.einsum(
            "rkgn,nkd->rkgd",
            weights.astype(jnp.bfloat16),
            value_block,
            preferred_element_type=jnp.float32,
        )
        return (top_new, total_new, numerator)

    initial = (
        jnp.full((tile_count, tile_rows, kv_heads, group_size), -1e30, jnp.float32),
        jnp.zeros((tile_count, tile_rows, kv_heads, group_size), jnp.float32),
        jnp.zeros((tile_count, tile_rows, kv_heads, group_size, head_width), jnp.float32),
    )
    key_piece = lax.all_gather(keys, "ctx", axis=0, tiled=True)
    value_piece = lax.all_gather(values, "ctx", axis=0, tiled=True)
    piece_rows = key_piece.shape[0]
    block_keys = piece_rows if piece_rows <= 512 else math.gcd(piece_rows, 512)
    block_count = piece_rows // block_keys

    def one_pair(turn, state_in):
        tile = turn // block_count
        offset = turn % block_count * block_keys
        key_block = lax.dynamic_slice_in_dim(key_piece, offset, block_keys, 0)
        value_block = lax.dynamic_slice_in_dim(value_piece, offset, block_keys, 0)
        key_places = offset + jnp.arange(block_keys, dtype=jnp.int32)
        query_tile = lax.dynamic_index_in_dim(grouped, tile, 0, keepdims=False)
        places_tile = lax.dynamic_index_in_dim(tile_places, tile, 0, keepdims=False)
        tile_state = tuple(
            (
                lax.dynamic_index_in_dim(part_state, tile, 0, keepdims=False)
                for part_state in state_in
            )
        )

        def compute(state_keep):
            fresh = absorb(state_keep, query_tile, places_tile, key_block, value_block, key_places)
            return tuple(
                (
                    lax.dynamic_update_index_in_dim(whole_state, new_part, tile, 0)
                    for whole_state, new_part in zip(state_in, fresh)
                )
            )

        return lax.cond(
            jnp.min(key_places) > tile_last[tile], lambda state_keep: state_in, compute, tile_state
        )

    top_final, total_final, numerator = lax.fori_loop(
        0, tile_count * block_count, one_pair, initial
    )
    attended = (
        (numerator / total_final[..., None])
        .reshape(row_count, kv_heads * group_size, head_width)
        .astype(jnp.bfloat16)
    )
    return attended


def solution(mesh):
    return jax.shard_map(
        local,
        mesh=mesh,
        in_specs=(
            P(("seq", "ctx"), "head", None),
            P(("seq", "ctx"), "head", None),
            P(("seq", "ctx"), "head", None),
        ),
        out_specs=P(("seq", "ctx"), "head", None),
        check_vma=False,
    )
```

profile of v0, /device:TPU:0, one launch (start us, length us, event | category | flops | bytes accessed | tf_op | source)
XLA Modules:
  0.0 48.2 jit_solution(4330699171862913210)
XLA Ops:
  0.1 0.8 %copy.11 = bf16[128,2,128]{2,0,1:T(8,128)(2,1)S(1)} copy(bf16[128,2,128]{2,1,0:T(2,128)(2,1)} %param.8) | data formatting | bytes 131072 | tf_op args[1]
  1.0 0.9 %copy.12 = bf16[128,2,128]{2,0,1:T(8,128)(2,1)S(1)} copy(bf16[128,2,128]{2,1,0:T(2,128)(2,1)} %param.9) | data formatting | bytes 131072 | tf_op args[2]
  1.8 7.2 %all_gather.7 = bf16[512,2,128]{2,0,1:T(8,128)(2,1)S(1)} all-gather(bf16[128,2,128]{2,0,1:T(8,128)(2,1)S(1)} %copy.12), channel_id=1, replica_groups=mesh['ctx'=4,'head'=2,'seq'=4] {'ctx'}, dimensions={0}, use_global_device_ids=true | all-gather | bytes 327680 | tf_op jit(solution)/shard_map/all_gather | solution.py:50
  9.1 5.8 %all_gather.6 = bf16[512,2,128]{2,0,1:T(8,128)(2,1)S(1)} all-gather(bf16[128,2,128]{2,0,1:T(8,128)(2,1)S(1)} %copy.11), channel_id=1, replica_groups=mesh['ctx'=4,'head'=2,'seq'=4] {'ctx'}, dimensions={0}, use_global_device_ids=true | all-gather | bytes 327680 | tf_op jit(solution)/shard_map/all_gather | solution.py:49
  14.9 2.4 %copy.13 = bf16[8,16,2,16,128]{4,3,1,2,0:T(8,128)(2,1)} copy(bf16[8,16,2,16,128]{4,3,2,1,0:T(8,128)(2,1)} %bitcast.69) | data formatting | bytes 2097152
  17.6 28.8 %while.21 = (s32[]{:T(128)}, f32[8,16,2,16]{3,1,2,0:T(8,128)S(1)}, f32[8,16,2,16]{3,1,2,0:T(8,128)S(1)}, f32[8,16,2,16,128]{4,3,1,2,0:T(8,128)S(1)}, s32[8]{0:T(...) while((s32[]{:T(128)}, f32[8,16,2,16]{3,1,2,0:T(8,128)S(1)}, ...), condition=%wide.region_6.7_spmd.clone, body=%wide.region_1.6_spmd.clone.sunk | while | flops 136719232 | bytes 5060129 | solution.py:83
  17.6 0.6 %dynamic_slice.109 = s32[1]{0:T(128)} dynamic-slice(s32[8]{0:T(128)S(1)} %get-tuple-element.588, s32[]{:T(128)} %copy.30), dynamic_slice_sizes={1} | dynamic-slice | bytes 12 | tf_op jit(solution)/shard_map/while/body/eval_jaxpr/dynamic_slice | solution.py:80
  18.9 2.3 %conditional.3 = ((f32[8,16,2,16]{3,1,2,0:T(8,128)S(1)}, f32[8,16,2,16]{3,1,2,0:T(8,128)S(1)}, f32[8,16,2,16,128]{4,3,1,2,0:T(8,128)S(1)})) conditional(s32[]{:T(128)} %bitcast.68, (f32[8,16,2,16]{3,1,2,0:T(8,128)S(1)}, s32[]{:T(128)}, s32[512]{0:T(512)S(1)}, s32[]{:T(128)}, bf16[8,16,2,16,128]{4,3,1,2,0:T(8,128)(2,1)}, ...), branch_computations={%region_2.4_spmd.clone, %region_5.5_spmd} | conditional | flops 136719232 | bytes 5056802 | solution.py:79
  19.0 1.3 %fusion.24 = (f32[16,2,16]{2,0,1:T(8,128)S(1)}, f32[16,2,16,512]{3,2,0,1:T(8,128)S(1)}) fusion(bf16[512,2,128]{2,0,1:T(8,128)(2,1)S(1)} %get-tuple-element.451, bf16[8,16,2,16,128]{4,3,1,2,0:T(8,128)(2,1)} %get-tuple-element.450, s32[]{:T(128)} %get-tuple-element.448, pred[16,512]{1,0:T(8,128)(4,1)S(1)} %broadcast_compare_fusion), kind=kOutput, calls=%fused_computation.38 | convolution fusion | flops 67894784 | bytes 1452544 | tf_op jit(solution)/shard_map/while/body/eval_jaxpr/cond/branch_0_fun/rkgd,nkd->rkgn/dot_general | solution.py:27
  20.3 0.4 fusion.8
  20.8 0.4 fusion.6
  21.2 0.6 %dynamic_slice.109 = s32[1]{0:T(128)} dynamic-slice(s32[8]{0:T(128)S(1)} %get-tuple-element.588, s32[]{:T(128)} %copy.30), dynamic_slice_sizes={1} | dynamic-slice | bytes 12 | tf_op jit(solution)/shard_map/while/body/eval_jaxpr/dynamic_slice | solution.py:80
  22.5 2.3 %conditional.3 = ((f32[8,16,2,16]{3,1,2,0:T(8,128)S(1)}, f32[8,16,2,16]{3,1,2,0:T(8,128)S(1)}, f32[8,16,2,16,128]{4,3,1,2,0:T(8,128)S(1)})) conditional(s32[]{:T(128)} %bitcast.68, (f32[8,16,2,16]{3,1,2,0:T(8,128)S(1)}, s32[]{:T(128)}, s32[512]{0:T(512)S(1)}, s32[]{:T(128)}, bf16[8,16,2,16,128]{4,3,1,2,0:T(8,128)(2,1)}, ...), branch_computations={%region_2.4_spmd.clone, %region_5.5_spmd} | conditional | flops 136719232 | bytes 5056802 | solution.py:79
  22.6 1.3 %fusion.24 = (f32[16,2,16]{2,0,1:T(8,128)S(1)}, f32[16,2,16,512]{3,2,0,1:T(8,128)S(1)}) fusion(bf16[512,2,128]{2,0,1:T(8,128)(2,1)S(1)} %get-tuple-element.451, bf16[8,16,2,16,128]{4,3,1,2,0:T(8,128)(2,1)} %get-tuple-element.450, s32[]{:T(128)} %get-tuple-element.448, pred[16,512]{1,0:T(8,128)(4,1)S(1)} %broadcast_compare_fusion), kind=kOutput, calls=%fused_computation.38 | convolution fusion | flops 67894784 | bytes 1452544 | tf_op jit(solution)/shard_map/while/body/eval_jaxpr/cond/branch_0_fun/rkgd,nkd->rkgn/dot_general | solution.py:27
  23.9 0.4 fusion.8
  24.3 0.4 fusion.6
  24.8 0.6 %dynamic_slice.109 = s32[1]{0:T(128)} dynamic-slice(s32[8]{0:T(128)S(1)} %get-tuple-element.588, s32[]{:T(128)} %copy.30), dynamic_slice_sizes={1} | dynamic-slice | bytes 12 | tf_op jit(solution)/shard_map/while/body/eval_jaxpr/dynamic_slice | solution.py:80
  26.0 2.3 %conditional.3 = ((f32[8,16,2,16]{3,1,2,0:T(8,128)S(1)}, f32[8,16,2,16]{3,1,2,0:T(8,128)S(1)}, f32[8,16,2,16,128]{4,3,1,2,0:T(8,128)S(1)})) conditional(s32[]{:T(128)} %bitcast.68, (f32[8,16,2,16]{3,1,2,0:T(8,128)S(1)}, s32[]{:T(128)}, s32[512]{0:T(512)S(1)}, s32[]{:T(128)}, bf16[8,16,2,16,128]{4,3,1,2,0:T(8,128)(2,1)}, ...), branch_computations={%region_2.4_spmd.clone, %region_5.5_spmd} | conditional | flops 136719232 | bytes 5056802 | solution.py:79
  26.2 1.3 %fusion.24 = (f32[16,2,16]{2,0,1:T(8,128)S(1)}, f32[16,2,16,512]{3,2,0,1:T(8,128)S(1)}) fusion(bf16[512,2,128]{2,0,1:T(8,128)(2,1)S(1)} %get-tuple-element.451, bf16[8,16,2,16,128]{4,3,1,2,0:T(8,128)(2,1)} %get-tuple-element.450, s32[]{:T(128)} %get-tuple-element.448, pred[16,512]{1,0:T(8,128)(4,1)S(1)} %broadcast_compare_fusion), kind=kOutput, calls=%fused_computation.38 | convolution fusion | flops 67894784 | bytes 1452544 | tf_op jit(solution)/shard_map/while/body/eval_jaxpr/cond/branch_0_fun/rkgd,nkd->rkgn/dot_general | solution.py:27
  27.5 0.4 fusion.8
  27.9 0.4 fusion.6
  28.4 0.6 %dynamic_slice.109 = s32[1]{0:T(128)} dynamic-slice(s32[8]{0:T(128)S(1)} %get-tuple-element.588, s32[]{:T(128)} %copy.30), dynamic_slice_sizes={1} | dynamic-slice | bytes 12 | tf_op jit(solution)/shard_map/while/body/eval_jaxpr/dynamic_slice | solution.py:80
  29.6 2.3 %conditional.3 = ((f32[8,16,2,16]{3,1,2,0:T(8,128)S(1)}, f32[8,16,2,16]{3,1,2,0:T(8,128)S(1)}, f32[8,16,2,16,128]{4,3,1,2,0:T(8,128)S(1)})) conditional(s32[]{:T(128)} %bitcast.68, (f32[8,16,2,16]{3,1,2,0:T(8,128)S(1)}, s32[]{:T(128)}, s32[512]{0:T(512)S(1)}, s32[]{:T(128)}, bf16[8,16,2,16,128]{4,3,1,2,0:T(8,128)(2,1)}, ...), branch_computations={%region_2.4_spmd.clone, %region_5.5_spmd} | conditional | flops 136719232 | bytes 5056802 | solution.py:79
  29.8 1.3 %fusion.24 = (f32[16,2,16]{2,0,1:T(8,128)S(1)}, f32[16,2,16,512]{3,2,0,1:T(8,128)S(1)}) fusion(bf16[512,2,128]{2,0,1:T(8,128)(2,1)S(1)} %get-tuple-element.451, bf16[8,16,2,16,128]{4,3,1,2,0:T(8,128)(2,1)} %get-tuple-element.450, s32[]{:T(128)} %get-tuple-element.448, pred[16,512]{1,0:T(8,128)(4,1)S(1)} %broadcast_compare_fusion), kind=kOutput, calls=%fused_computation.38 | convolution fusion | flops 67894784 | bytes 1452544 | tf_op jit(solution)/shard_map/while/body/eval_jaxpr/cond/branch_0_fun/rkgd,nkd->rkgn/dot_general | solution.py:27
  31.1 0.4 fusion.8
  31.5 0.4 fusion.6
  32.0 0.6 %dynamic_slice.109 = s32[1]{0:T(128)} dynamic-slice(s32[8]{0:T(128)S(1)} %get-tuple-element.588, s32[]{:T(128)} %copy.30), dynamic_slice_sizes={1} | dynamic-slice | bytes 12 | tf_op jit(solution)/shard_map/while/body/eval_jaxpr/dynamic_slice | solution.py:80
  33.2 2.3 %conditional.3 = ((f32[8,16,2,16]{3,1,2,0:T(8,128)S(1)}, f32[8,16,2,16]{3,1,2,0:T(8,128)S(1)}, f32[8,16,2,16,128]{4,3,1,2,0:T(8,128)S(1)})) conditional(s32[]{:T(128)} %bitcast.68, (f32[8,16,2,16]{3,1,2,0:T(8,128)S(1)}, s32[]{:T(128)}, s32[512]{0:T(512)S(1)}, s32[]{:T(128)}, bf16[8,16,2,16,128]{4,3,1,2,0:T(8,128)(2,1)}, ...), branch_computations={%region_2.4_spmd.clone, %region_5.5_spmd} | conditional | flops 136719232 | bytes 5056802 | solution.py:79
  33.4 1.3 %fusion.24 = (f32[16,2,16]{2,0,1:T(8,128)S(1)}, f32[16,2,16,512]{3,2,0,1:T(8,128)S(1)}) fusion(bf16[512,2,128]{2,0,1:T(8,128)(2,1)S(1)} %get-tuple-element.451, bf16[8,16,2,16,128]{4,3,1,2,0:T(8,128)(2,1)} %get-tuple-element.450, s32[]{:T(128)} %get-tuple-element.448, pred[16,512]{1,0:T(8,128)(4,1)S(1)} %broadcast_compare_fusion), kind=kOutput, calls=%fused_computation.38 | convolution fusion | flops 67894784 | bytes 1452544 | tf_op jit(solution)/shard_map/while/body/eval_jaxpr/cond/branch_0_fun/rkgd,nkd->rkgn/dot_general | solution.py:27
  34.7 0.4 fusion.8
  35.1 0.4 fusion.6
  35.5 0.6 %dynamic_slice.109 = s32[1]{0:T(128)} dynamic-slice(s32[8]{0:T(128)S(1)} %get-tuple-element.588, s32[]{:T(128)} %copy.30), dynamic_slice_sizes={1} | dynamic-slice | bytes 12 | tf_op jit(solution)/shard_map/while/body/eval_jaxpr/dynamic_slice | solution.py:80
  36.8 2.3 %conditional.3 = ((f32[8,16,2,16]{3,1,2,0:T(8,128)S(1)}, f32[8,16,2,16]{3,1,2,0:T(8,128)S(1)}, f32[8,16,2,16,128]{4,3,1,2,0:T(8,128)S(1)})) conditional(s32[]{:T(128)} %bitcast.68, (f32[8,16,2,16]{3,1,2,0:T(8,128)S(1)}, s32[]{:T(128)}, s32[512]{0:T(512)S(1)}, s32[]{:T(128)}, bf16[8,16,2,16,128]{4,3,1,2,0:T(8,128)(2,1)}, ...), branch_computations={%region_2.4_spmd.clone, %region_5.5_spmd} | conditional | flops 136719232 | bytes 5056802 | solution.py:79
  37.0 1.3 %fusion.24 = (f32[16,2,16]{2,0,1:T(8,128)S(1)}, f32[16,2,16,512]{3,2,0,1:T(8,128)S(1)}) fusion(bf16[512,2,128]{2,0,1:T(8,128)(2,1)S(1)} %get-tuple-element.451, bf16[8,16,2,16,128]{4,3,1,2,0:T(8,128)(2,1)} %get-tuple-element.450, s32[]{:T(128)} %get-tuple-element.448, pred[16,512]{1,0:T(8,128)(4,1)S(1)} %broadcast_compare_fusion), kind=kOutput, calls=%fused_computation.38 | convolution fusion | flops 67894784 | bytes 1452544 | tf_op jit(solution)/shard_map/while/body/eval_jaxpr/cond/branch_0_fun/rkgd,nkd->rkgn/dot_general | solution.py:27
  38.3 0.4 fusion.8
  38.7 0.4 fusion.6
  39.1 0.6 %dynamic_slice.109 = s32[1]{0:T(128)} dynamic-slice(s32[8]{0:T(128)S(1)} %get-tuple-element.588, s32[]{:T(128)} %copy.30), dynamic_slice_sizes={1} | dynamic-slice | bytes 12 | tf_op jit(solution)/shard_map/while/body/eval_jaxpr/dynamic_slice | solution.py:80
  40.4 2.3 %conditional.3 = ((f32[8,16,2,16]{3,1,2,0:T(8,128)S(1)}, f32[8,16,2,16]{3,1,2,0:T(8,128)S(1)}, f32[8,16,2,16,128]{4,3,1,2,0:T(8,128)S(1)})) conditional(s32[]{:T(128)} %bitcast.68, (f32[8,16,2,16]{3,1,2,0:T(8,128)S(1)}, s32[]{:T(128)}, s32[512]{0:T(512)S(1)}, s32[]{:T(128)}, bf16[8,16,2,16,128]{4,3,1,2,0:T(8,128)(2,1)}, ...), branch_computations={%region_2.4_spmd.clone, %region_5.5_spmd} | conditional | flops 136719232 | bytes 5056802 | solution.py:79
  40.6 1.3 %fusion.24 = (f32[16,2,16]{2,0,1:T(8,128)S(1)}, f32[16,2,16,512]{3,2,0,1:T(8,128)S(1)}) fusion(bf16[512,2,128]{2,0,1:T(8,128)(2,1)S(1)} %get-tuple-element.451, bf16[8,16,2,16,128]{4,3,1,2,0:T(8,128)(2,1)} %get-tuple-element.450, s32[]{:T(128)} %get-tuple-element.448, pred[16,512]{1,0:T(8,128)(4,1)S(1)} %broadcast_compare_fusion), kind=kOutput, calls=%fused_computation.38 | convolution fusion | flops 67894784 | bytes 1452544 | tf_op jit(solution)/shard_map/while/body/eval_jaxpr/cond/branch_0_fun/rkgd,nkd->rkgn/dot_general | solution.py:27
  41.9 0.4 fusion.8
  42.3 0.4 fusion.6
  42.7 0.6 %dynamic_slice.109 = s32[1]{0:T(128)} dynamic-slice(s32[8]{0:T(128)S(1)} %get-tuple-element.588, s32[]{:T(128)} %copy.30), dynamic_slice_sizes={1} | dynamic-slice | bytes 12 | tf_op jit(solution)/shard_map/while/body/eval_jaxpr/dynamic_slice | solution.py:80
  44.0 2.3 %conditional.3 = ((f32[8,16,2,16]{3,1,2,0:T(8,128)S(1)}, f32[8,16,2,16]{3,1,2,0:T(8,128)S(1)}, f32[8,16,2,16,128]{4,3,1,2,0:T(8,128)S(1)})) conditional(s32[]{:T(128)} %bitcast.68, (f32[8,16,2,16]{3,1,2,0:T(8,128)S(1)}, s32[]{:T(128)}, s32[512]{0:T(512)S(1)}, s32[]{:T(128)}, bf16[8,16,2,16,128]{4,3,1,2,0:T(8,128)(2,1)}, ...), branch_computations={%region_2.4_spmd.clone, %region_5.5_spmd} | conditional | flops 136719232 | bytes 5056802 | solution.py:79
  44.2 1.3 %fusion.24 = (f32[16,2,16]{2,0,1:T(8,128)S(1)}, f32[16,2,16,512]{3,2,0,1:T(8,128)S(1)}) fusion(bf16[512,2,128]{2,0,1:T(8,128)(2,1)S(1)} %get-tuple-element.451, bf16[8,16,2,16,128]{4,3,1,2,0:T(8,128)(2,1)} %get-tuple-element.450, s32[]{:T(128)} %get-tuple-element.448, pred[16,512]{1,0:T(8,128)(4,1)S(1)} %broadcast_compare_fusion), kind=kOutput, calls=%fused_computation.38 | convolution fusion | flops 67894784 | bytes 1452544 | tf_op jit(solution)/shard_map/while/body/eval_jaxpr/cond/branch_0_fun/rkgd,nkd->rkgn/dot_general | solution.py:27
  45.5 0.4 fusion.8
  45.9 0.4 fusion.6
  46.3 0.7 %divide_convert_fusion = bf16[8,16,2,16,128]{4,3,1,2,0:T(8,128)(2,1)S(1)} fusion(f32[8,16,2,16,128]{4,3,1,2,0:T(8,128)S(1)} %get-tuple-element.395, f32[8,16,2,16]{3,1,2,0:T(8,128)S(1)} %get-tuple-element.396), kind=kLoop, calls=%fused_computation.36 | loop fusion | flops 1048576 | bytes 3162112 | tf_op jit(solution)/shard_map/convert_element_type | solution.py:89
  47.1 1.2 %copy.14 = bf16[8,16,2,16,128]{4,3,2,1,0:T(8,128)(2,1)} copy(bf16[8,16,2,16,128]{4,3,1,2,0:T(8,128)(2,1)S(1)} %divide_convert_fusion) | data formatting | bytes 2097152 | tf_op jit(solution)/shard_map/convert_element_type | solution.py:89
  (84 shorter events, 1.8 us)
where the time goes:
time: 48.7 us; the launch traced here: 48.2 us
  matrix products  13.4 us (28%)
  blocking collectives  13.1 us (27%)
  local copies, waits for them, and re-layouts  10.9 us (22%)
  loops' own time  6.19 us (13%)
  other arithmetic  4.63 us (10%)
    dot_general x8, matrix products, absorb(): jnp.einsum('rkgd,nkd->rkgn', query_tile, key_block, preferred_element_typ...  10.4 us
    all_gather x1, blocking collectives, local(): value_piece = lax.all_gather(values, 'ctx', axis=0, tiled=True)  7.22 us
    all_gather x1, blocking collectives, local(): key_piece = lax.all_gather(keys, 'ctx', axis=0, tiled=True)  5.85 us
    another operation x1, loops' own time, local(): lax.fori_loop(0, tile_count * block_count, one_pair, initial)  5.5 us
    dynamic_slice x8, local copies, waits for them, and re-layouts, one_pair(): tile_last[tile]  4.9 us
    unnamed x3, local copies, waits for them, and re-layouts  4.12 us
    dot_general x8, matrix products, absorb(): jnp.einsum('rkgn,nkd->rkgd', weights.astype(jnp.bfloat16), value_block, p...  3.05 us
    reduce_sum x8, other arithmetic, absorb(): total_new = total_old * rescale + jnp.sum(weights, axis=-1)  2.83 us

commit v1 on v0

v1 whole, which is shorter than its diff:
```python
import functools
import math

import jax
import jax.numpy as jnp
from jax import lax
from jax.experimental import pallas as pl
from jax.experimental.pallas import tpu as pltpu
from jax.sharding import PartitionSpec as P

VMEM_LIMIT = 30 * 1024 * 1024
TILE_ROWS = 256
NEG = -1e30


def tile_plan(rows, group):
    return math.gcd(rows, max(1, TILE_ROWS // group))


def split_into(packed, kv_heads, base, block_ref):
    total, depth = packed.shape
    count = total // kv_heads
    if kv_heads == 1:
        block_ref[0, base : base + count, :depth] = packed
        return
    rows = lax.broadcasted_iota(jnp.int32, (count, total), 0)
    cols = lax.broadcasted_iota(jnp.int32, (count, total), 1)
    for head in range(kv_heads):
        pick = (cols == rows * kv_heads + head).astype(packed.dtype)
        block = jnp.dot(pick, packed, preferred_element_type=jnp.float32)
        block_ref[head, base : base + count, :depth] = block.astype(packed.dtype)


def fill_ones(values_ref, depth):
    shape = (values_ref.shape[0], values_ref.shape[1], values_ref.shape[2] - depth)
    values_ref[:, :, depth:] = jnp.ones(shape, values_ref.dtype)


def tile_queries(q_ref, head, group, tile, positions):
    rows = q_ref[tile * positions : (tile + 1) * positions, head * group : (head + 1) * group, :]
    return rows.reshape(positions * group, q_ref.shape[2])


def scores_of(q_rows, keys):
    return lax.dot_general(
        q_rows, keys, (((1,), (1,)), ((), ())), preferred_element_type=jnp.float32
    )


def put_result(stage_ref, head, group, tile, positions, numer, total):
    result = (numer * (1.0 / total)).astype(stage_ref.dtype)
    stage_ref[tile * positions : (tile + 1) * positions, head * group : (head + 1) * group, :] = (
        result.reshape(positions, group, numer.shape[1])
    )


def out_copy(stage_ref, out_ref, sems, tile, positions):
    where = pl.ds(tile * positions, positions)
    return pltpu.make_async_copy(stage_ref.at[where], out_ref.at[where], sems.at[tile])


def first_kernel(axis, pair, kv_heads, factor, *refs):
    q_hbm, k_hbm, v_hbm = refs[:3]
    near_refs = refs[3 : 1 + 2 * pair]
    q_ref, top_ref, sums_ref, out_ref = refs[1 + 2 * pair : 5 + 2 * pair]
    own_k, own_v, keys_ref, values_ref, stage_ref, kv_sems, q_sems, out_sems = refs[5 + 2 * pair :]
    rows, heads, depth = q_ref.shape
    group = heads // kv_heads
    positions = tile_plan(rows, group)
    tile_rows = positions * group
    tiles = rows // positions
    me = lax.axis_index(axis)
    lane = lax.rem(me, pair)

    copy_k = pltpu.make_async_copy(k_hbm, own_k, kv_sems.at[0])
    copy_v = pltpu.make_async_copy(v_hbm, own_v, kv_sems.at[1])
    copy_q = pltpu.make_async_copy(q_hbm, q_ref, q_sems.at[0])
    copy_k.start()
    copy_v.start()
    copy_q.start()
    fill_ones(values_ref, depth)
    if pair > 1:
        split_into(near_refs[0][...], kv_heads, rows, keys_ref)
        split_into(near_refs[1][...], kv_heads, rows, values_ref)
    copy_k.wait()
    split_into(own_k[...], kv_heads, 0, keys_ref)
    copy_v.wait()
    split_into(own_v[...], kv_heads, 0, values_ref)
    copy_q.wait()
    bias = jnp.where(lane > 0, 0.0, NEG).astype(jnp.float32)

    for tile in range(tiles):
        for head in range(kv_heads):
            where = slice(tile * tile_rows, (tile + 1) * tile_rows)
            q_rows = tile_queries(q_ref, head, group, tile, positions)
            scores = scores_of(q_rows, keys_ref[head])
            own = scores[:, :rows].reshape(positions, group, rows)
            place = tile * positions + lax.broadcasted_iota(jnp.int32, own.shape, 0)
            own = jnp.where(lax.broadcasted_iota(jnp.int32, own.shape, 2) <= place, own, NEG)
            own = own.reshape(tile_rows, rows)
            if pair > 1:
                scores = jnp.concatenate([own, scores[:, rows:] + bias], axis=1)
            else:
                scores = own
            top = jnp.max(scores, axis=1, keepdims=True)
            weights = jnp.exp2((scores - top) * factor).astype(values_ref.dtype)
            top_ref[head, where, :] = jnp.broadcast_to(top, (tile_rows, depth))
            sums_ref[head, where, :] = jnp.dot(
                weights, values_ref[head], preferred_element_type=jnp.float32
            )

    @pl.when(lax.div(me, pair) == 0)
    def _():
        for tile in range(tiles):
            where = slice(tile * tile_rows, (tile + 1) * tile_rows)
            for head in range(kv_heads):
                put_result(
                    stage_ref, head, group, tile, positions,
                    sums_ref[head, where, :depth], sums_ref[head, where, depth:],
                )
            out_copy(stage_ref, out_ref, out_sems, tile, positions).start()
        for tile in range(tiles):
            out_copy(stage_ref, out_ref, out_sems, tile, positions).wait()


def last_kernel(axis, pair, kv_heads, factor, hop, *refs):
    q_ref = refs[0]
    far_refs = refs[1 : 1 + 2 * pair]
    top_ref, sums_ref = refs[1 + 2 * pair : 3 + 2 * pair]
    out_ref = refs[4 + 2 * pair]
    keys_ref, values_ref, stage_ref, out_sems = refs[5 + 2 * pair :]
    rows, heads, depth = q_ref.shape
    group = heads // kv_heads
    positions = tile_plan(rows, group)
    tile_rows = positions * group
    tiles = rows // positions
    me = lax.axis_index(axis)

    @pl.when(lax.div(me, pair) >= hop)
    def _():
        fill_ones(values_ref, depth)
        for block in range(pair):
            split_into(far_refs[2 * block][...], kv_heads, block * rows, keys_ref)
            split_into(far_refs[2 * block + 1][...], kv_heads, block * rows, values_ref)

        for tile in range(tiles):
            where = slice(tile * tile_rows, (tile + 1) * tile_rows)
            for head in range(kv_heads):
                q_rows = tile_queries(q_ref, head, group, tile, positions)
                scores = scores_of(q_rows, keys_ref[head])
                old = top_ref[head, where, :]
                top = jnp.maximum(jnp.max(scores, axis=1, keepdims=True), old)
                weights = jnp.concatenate(
                    [
                        jnp.exp2((scores[:, at : at + depth] - top) * factor)
                        for at in range(0, scores.shape[1], depth)
                    ],
                    axis=1,
                ).astype(values_ref.dtype)
                rescale = jnp.exp2((old - top) * factor)
                sums = jnp.dot(weights, values_ref[head], preferred_element_type=jnp.float32)
                put_result(
                    stage_ref, head, group, tile, positions,
                    sums_ref[head, where, :depth] * rescale + sums[:, :depth],
                    sums_ref[head, where, depth:] * rescale + sums[:, depth:],
                )
            out_copy(stage_ref, out_ref, out_sems, tile, positions).start()
        for tile in range(tiles):
            out_copy(stage_ref, out_ref, out_sems, tile, positions).wait()


def in_vmem(array):
    return pltpu.with_memory_space_constraint(array, pltpu.VMEM)


def in_hbm(array):
    return pltpu.with_memory_space_constraint(array, pltpu.HBM)


def local(ctx_size, queries, keys, values):
    rows, heads, depth = queries.shape
    kv_heads = keys.shape[1]
    group = heads // kv_heads
    pair = 2 if ctx_size % 2 == 0 else 1
    chips = ctx_size // pair
    factor = math.log2(math.e) / math.sqrt(depth)
    vmem = pl.BlockSpec(memory_space=pltpu.VMEM)
    anywhere = pl.BlockSpec(memory_space=pl.ANY)

    keys = keys.reshape(rows * kv_heads, depth)
    values = values.reshape(rows * kv_heads, depth)
    swap = [(i, i ^ 1) for i in range(ctx_size)]
    hops = [
        [
            (i, (i // pair + hop) % chips * pair + (pair - 1 - i % pair))
            for i in range(ctx_size)
        ]
        for hop in range(chips)
    ]

    far_keys = lax.ppermute(keys, "ctx", hops[1])
    far_values = lax.ppermute(values, "ctx", hops[1])
    near = []
    if pair == 2:
        near = [lax.ppermute(keys, "ctx", swap), lax.ppermute(values, "ctx", swap)]

    positions = tile_plan(rows, group)
    tiles = rows // positions
    work = heads * rows * rows * pair
    cost = pl.CostEstimate(
        flops=work * depth * 4, bytes_accessed=heads * rows * depth * 2, transcendentals=work
    )
    split_scratch = [
        pltpu.VMEM((kv_heads, pair * rows, depth), keys.dtype),
        pltpu.VMEM((kv_heads, pair * rows, 2 * depth), keys.dtype),
        pltpu.VMEM(queries.shape, queries.dtype),
    ]
    q_vmem, top, sums, out = pl.pallas_call(
        functools.partial(first_kernel, "ctx", pair, kv_heads, factor),
        out_shape=(
            pltpu.VMEM(queries.shape, queries.dtype),
            pltpu.VMEM((kv_heads, rows * group, depth), jnp.float32),
            pltpu.VMEM((kv_heads, rows * group, 2 * depth), jnp.float32),
            jax.ShapeDtypeStruct(queries.shape, queries.dtype),
        ),
        in_specs=[anywhere] * 3 + [vmem] * len(near),
        out_specs=(vmem,) * 3 + (anywhere,),
        scratch_shapes=[
            pltpu.VMEM(keys.shape, keys.dtype),
            pltpu.VMEM(keys.shape, keys.dtype),
            *split_scratch,
            pltpu.SemaphoreType.DMA((2,)),
            pltpu.SemaphoreType.DMA((1,)),
            pltpu.SemaphoreType.DMA((tiles,)),
        ],
        compiler_params=pltpu.CompilerParams(vmem_limit_bytes=VMEM_LIMIT),
        cost_estimate=cost,
    )(*[in_hbm(x) for x in (queries, keys, values)], *[in_vmem(x) for x in near])

    far_keys, top = lax.optimization_barrier((far_keys, top))
    far_values, sums = lax.optimization_barrier((far_values, sums))
    far = [far_keys, far_values]
    if pair == 2:
        far += [lax.ppermute(far_keys, "ctx", swap), lax.ppermute(far_values, "ctx", swap)]
    return pl.pallas_call(
        functools.partial(last_kernel, "ctx", pair, kv_heads, factor, 1),
        out_shape=jax.ShapeDtypeStruct(queries.shape, queries.dtype),
        in_specs=[vmem] * (3 + 2 * pair) + [anywhere],
        out_specs=anywhere,
        scratch_shapes=[*split_scratch, pltpu.SemaphoreType.DMA((tiles,))],
        input_output_aliases={3 + 2 * pair: 0},
        compiler_params=pltpu.CompilerParams(vmem_limit_bytes=VMEM_LIMIT),
        cost_estimate=cost,
    )(in_vmem(q_vmem), *[in_vmem(x) for x in far], *[in_vmem(x) for x in (top, sums)], in_hbm(out))


def solution(mesh):
    return jax.shard_map(
        functools.partial(local, mesh.shape["ctx"]),
        mesh=mesh,
        in_specs=(
            P(("seq", "ctx"), "head", None),
            P(("seq", "ctx"), "head", None),
            P(("seq", "ctx"), "head", None),
        ),
        out_specs=P(("seq", "ctx"), "head", None),
        check_vma=False,
    )
```

time: 48.7 us -> 11 us (0.23)
  the two profiles are of different devices: /device:TPU:0 before, /device:TPU:7 now
where the time goes in v1:
time: 11 us; the launch traced here: 10.9 us
  Pallas kernels  5.56 us (51%)
  starting transfers between devices  2.93 us (27%)
  waiting for transfers between devices  2.38 us (22%)
    pallas_call x1, Pallas kernels, local(): pl.pallas_call(functools.partial(first_kernel, 'ctx', pair, kv_heads, fac...  2.93 us
    pallas_call x1, Pallas kernels, local(): pl.pallas_call(functools.partial(last_kernel, 'ctx', pair, kv_heads, fact...  2.63 us
    ppermute x1, starting transfers between devices, local(): far_values = lax.ppermute(values, 'ctx', hops[1])  1.13 us
    ppermute x1, waiting for transfers between devices, local(): far_values = lax.ppermute(values, 'ctx', hops[1])  1.04 us
    ppermute x1, waiting for transfers between devices, local(): lax.ppermute(far_values, 'ctx', swap)  0.79 us
    ppermute x2, starting transfers between devices, local(): near = [lax.ppermute(keys, 'ctx', swap), lax.ppermute(values, 'ctx', swap)]  0.68 us
    ppermute x1, starting transfers between devices, local(): far_keys = lax.ppermute(keys, 'ctx', hops[1])  0.62 us
    ppermute x1, starting transfers between devices, local(): lax.ppermute(far_values, 'ctx', swap)  0.39 us
  transfers between devices with their start and end apart: 6, of which 4 were waited for; matrix products, arithmetic and copies ran while one was open for 0% of the time, Pallas kernels for 27%

profile of v1, /device:TPU:7, one launch (start us, length us, event | category | flops | bytes accessed | tf_op | source)
XLA Modules:
  0.0 10.9 jit_solution(7769974996242366575)
XLA Ops:
  0.0 0.7 %collective-permute-start = (bf16[256,128]{1,0:T(8,128)(2,1)}, bf16[256,128]{1,0:T(8,128)(2,1)S(1)}, u32[]{:S(2)}, u32[]{:S(2)}) collective-permute-start(bf16[256,128]{1,0:T(8,128)(2,1)} %bitcast.2), channel_id=1, source_target_pairs={{0,8},{8,0},{16,24},{24,16},{1,9},{9,1},{17,25},{25,17},{2,10},{10... | collective-permute-start | bytes 196616 | tf_op jit(solution)/shard_map/ppermute | solution.py:205
  0.7 0.0 collective-permute-start.1
  0.7 0.6 %collective-permute-start.2 = (bf16[256,128]{1,0:T(8,128)(2,1)}, bf16[256,128]{1,0:T(8,128)(2,1)S(1)}, u32[]{:S(2)}, u32[]{:S(2)}) collective-permute-start(bf16[256,128]{1,0:T(8,128)(2,1)} %bitcast.3), channel_id=1, source_target_pairs={{0,24},{8,16},{16,8},{24,0},{1,25},{9,17},{17,9},{25,1},{2,26},{10... | collective-permute-start | bytes 196616 | tf_op jit(solution)/shard_map/ppermute | solution.py:201
  1.3 1.1 %collective-permute-start.3 = (bf16[256,128]{1,0:T(8,128)(2,1)}, bf16[256,128]{1,0:T(8,128)(2,1)S(1)}, u32[]{:S(2)}, u32[]{:S(2)}) collective-permute-start(bf16[256,128]{1,0:T(8,128)(2,1)} %bitcast.6), channel_id=1, source_target_pairs={{0,24},{8,16},{16,8},{24,0},{1,25},{9,17},{17,9},{25,1},{2,26},{10... | collective-permute-start | bytes 196616 | tf_op jit(solution)/shard_map/ppermute | solution.py:202
  2.4 0.0 collective-permute-done.refs_3_
  2.4 0.0 collective-permute-done.1.refs_4_
  2.4 2.9 %shard_map.37 = (bf16[128,32,128]{2,1,0:T(8,128)(2,1)S(1)}, f32[2,2048,128]{2,1,0:T(8,128)S(1)}, f32[2,2048,256]{2,1,0:T(8,128)S(1)}, bf16[128,32,128]{2,1,0:T(8,128)(2,1)}) custom-call(bf16[128,32,128]{2,1,0:T(8,128)(2,1)} %refs_0_.1, bf16[256,128]{1,0:T(8,128)(2,1)} %bitcast.4, bf16[256,128]{1,0:T(8,128)(2,1)} %bitcast.7, ...), custom_call_target="tpu_custom_call" | custom-call | flops 536870912 | bytes 1048576 | tf_op jit(solution)/shard_map/pallas_call | solution.py:218
  5.4 0.2 %collective-permute-done.2.refs_1_ = bf16[256,128]{1,0:T(8,128)(2,1)S(1)} collective-permute-done((bf16[256,128]{1,0:T(8,128)(2,1)}, bf16[256,128]{1,0:T(8,128)(2,1)S(1)}, u32[]{:S(2)}, u32[]{:S(2)}) %collective-permute-start.2) | collective-permute-done | bytes 65568 | tf_op jit(solution)/shard_map/ppermute | solution.py:201
  5.6 1.0 %collective-permute-done.3.refs_2_ = bf16[256,128]{1,0:T(8,128)(2,1)S(1)} collective-permute-done((bf16[256,128]{1,0:T(8,128)(2,1)}, bf16[256,128]{1,0:T(8,128)(2,1)S(1)}, u32[]{:S(2)}, u32[]{:S(2)}) %collective-permute-start.3) | collective-permute-done | bytes 65568 | tf_op jit(solution)/shard_map/ppermute | solution.py:202
  6.6 0.4 %collective-permute-start.5 = (bf16[256,128]{1,0:T(8,128)(2,1)S(1)}, bf16[256,128]{1,0:T(8,128)(2,1)S(1)}, u32[]{:S(2)}, u32[]{:S(2)}) collective-permute-start(bf16[256,128]{1,0:T(8,128)(2,1)S(1)} %collective-permute-done.3.refs_2_), channel_id=1, source_target_pairs={{0,8},{8,0},{16,24},{24,16},{1,9},{9,1},{17,25},{25,17},{2,10},{10... | collective-permute-start | bytes 196616 | tf_op jit(solution)/shard_map/ppermute | solution.py:244
  7.0 0.1 %collective-permute-start.4 = (bf16[256,128]{1,0:T(8,128)(2,1)S(1)}, bf16[256,128]{1,0:T(8,128)(2,1)S(1)}, u32[]{:S(2)}, u32[]{:S(2)}) collective-permute-start(bf16[256,128]{1,0:T(8,128)(2,1)S(1)} %collective-permute-done.2.refs_1_), channel_id=1, source_target_pairs={{0,8},{8,0},{16,24},{24,16},{1,9},{9,1},{17,25},{25,17},{2,10},{10... | collective-permute-start | bytes 196616 | tf_op jit(solution)/shard_map/ppermute | solution.py:244
  7.1 0.8 %collective-permute-done.5.refs_4_ = bf16[256,128]{1,0:T(8,128)(2,1)S(1)} collective-permute-done((bf16[256,128]{1,0:T(8,128)(2,1)S(1)}, bf16[256,128]{1,0:T(8,128)(2,1)S(1)}, u32[]{:S(2)}, u32[]{:S(2)}) %collective-permute-start.5) | collective-permute-done | bytes 65568 | tf_op jit(solution)/shard_map/ppermute | solution.py:244
  7.9 0.4 %collective-permute-done.4.refs_3_ = bf16[256,128]{1,0:T(8,128)(2,1)S(1)} collective-permute-done((bf16[256,128]{1,0:T(8,128)(2,1)S(1)}, bf16[256,128]{1,0:T(8,128)(2,1)S(1)}, u32[]{:S(2)}, u32[]{:S(2)}) %collective-permute-start.4) | collective-permute-done | bytes 65568 | tf_op jit(solution)/shard_map/ppermute | solution.py:244
  8.3 2.6 %shard_map.38 = bf16[128,32,128]{2,1,0:T(8,128)(2,1)} custom-call(bf16[128,32,128]{2,1,0:T(8,128)(2,1)S(1)} %get-tuple-element.13.refs_0_, bf16[256,128]{1,0:T(8,128)(2,1)S(1)} %collective-permute-done.2.refs_1_, bf16[256,128]{1,0:T(8,128)(2,1)S(1)} %collective-permute-done.3.refs_2_, ...), custom_call_target="tpu_custom_call", output_to_operand_aliasing={{}: (7, {})} | custom-call | flops 536870912 | bytes 1048576 | tf_op jit(solution)/shard_map/pallas_call | solution.py:245
Async XLA Ops:
  0.0 2.4 %collective-permute-start = (bf16[256,128]{1,0:T(8,128)(2,1)}, bf16[256,128]{1,0:T(8,128)(2,1)S(1)}, u32[]{:S(2)}, u32[]{:S(2)}) collective-permute-start(bf16[256,128]{1,0:T(8,128)(2,1)} %bitcast.2), channel_id=1, source_target_pairs={{0,8},{8,0},{16,24},{24,16},{1,9},{9,1},{17,25},{25,17},{2,10},{10... | collective-permute-start | bytes 196616 | tf_op jit(solution)/shard_map/ppermute | solution.py:205
  0.7 1.8 %collective-permute-start.1 = (bf16[256,128]{1,0:T(8,128)(2,1)}, bf16[256,128]{1,0:T(8,128)(2,1)S(1)}, u32[]{:S(2)}, u32[]{:S(2)}) collective-permute-start(bf16[256,128]{1,0:T(8,128)(2,1)} %bitcast.5), channel_id=1, source_target_pairs={{0,8},{8,0},{16,24},{24,16},{1,9},{9,1},{17,25},{25,17},{2,10},{10... | collective-permute-start | bytes 196616 | tf_op jit(solution)/shard_map/ppermute | solution.py:205
  0.7 4.9 %collective-permute-start.2 = (bf16[256,128]{1,0:T(8,128)(2,1)}, bf16[256,128]{1,0:T(8,128)(2,1)S(1)}, u32[]{:S(2)}, u32[]{:S(2)}) collective-permute-start(bf16[256,128]{1,0:T(8,128)(2,1)} %bitcast.3), channel_id=1, source_target_pairs={{0,24},{8,16},{16,8},{24,0},{1,25},{9,17},{17,9},{25,1},{2,26},{10... | collective-permute-start | bytes 196616 | tf_op jit(solution)/shard_map/ppermute | solution.py:201
  1.3 5.3 %collective-permute-start.3 = (bf16[256,128]{1,0:T(8,128)(2,1)}, bf16[256,128]{1,0:T(8,128)(2,1)S(1)}, u32[]{:S(2)}, u32[]{:S(2)}) collective-permute-start(bf16[256,128]{1,0:T(8,128)(2,1)} %bitcast.6), channel_id=1, source_target_pairs={{0,24},{8,16},{16,8},{24,0},{1,25},{9,17},{17,9},{25,1},{2,26},{10... | collective-permute-start | bytes 196616 | tf_op jit(solution)/shard_map/ppermute | solution.py:202
  6.6 1.3 %collective-permute-start.5 = (bf16[256,128]{1,0:T(8,128)(2,1)S(1)}, bf16[256,128]{1,0:T(8,128)(2,1)S(1)}, u32[]{:S(2)}, u32[]{:S(2)}) collective-permute-start(bf16[256,128]{1,0:T(8,128)(2,1)S(1)} %collective-permute-done.3.refs_2_), channel_id=1, source_target_pairs={{0,8},{8,0},{16,24},{24,16},{1,9},{9,1},{17,25},{25,17},{2,10},{10... | collective-permute-start | bytes 196616 | tf_op jit(solution)/shard_map/ppermute | solution.py:244
  7.0 1.3 %collective-permute-start.4 = (bf16[256,128]{1,0:T(8,128)(2,1)S(1)}, bf16[256,128]{1,0:T(8,128)(2,1)S(1)}, u32[]{:S(2)}, u32[]{:S(2)}) collective-permute-start(bf16[256,128]{1,0:T(8,128)(2,1)S(1)} %collective-permute-done.2.refs_1_), channel_id=1, source_target_pairs={{0,8},{8,0},{16,24},{24,16},{1,9},{9,1},{17,25},{25,17},{2,10},{10... | collective-permute-start | bytes 196616 | tf_op jit(solution)/shard_map/ppermute | solution.py:244

commit v2 on v1

v2 whole, which is shorter than its diff:
```python
import functools
import math

import jax
import jax.numpy as jnp
from jax import lax
from jax.experimental import pallas as pl
from jax.experimental.pallas import tpu as pltpu
from jax.sharding import PartitionSpec as P

VMEM_LIMIT = 30 * 1024 * 1024
TILE_ROWS = 256
NEG = -1e30
DIRECT = False


def tile_plan(rows, group):
    return math.gcd(rows, max(1, TILE_ROWS // group))


def split_into(packed, kv_heads, base, wide_ref, block_ref):
    total, depth = packed.shape
    count = total // kv_heads
    if kv_heads == 1:
        block_ref[0, base : base + count, :depth] = packed
        return
    wide_ref[...] = packed.astype(jnp.float32)
    for head in range(kv_heads):
        block = wide_ref[pl.ds(head, count, stride=kv_heads), :]
        block_ref[head, base : base + count, :depth] = block.astype(packed.dtype)


def fill_ones(values_ref, depth):
    shape = (values_ref.shape[0], values_ref.shape[1], values_ref.shape[2] - depth)
    values_ref[:, :, depth:] = jnp.ones(shape, values_ref.dtype)


def tile_queries(q_ref, head, group, tile, positions):
    rows = q_ref[tile * positions : (tile + 1) * positions, head * group : (head + 1) * group, :]
    return rows.reshape(positions * group, q_ref.shape[2])


def scores_of(q_rows, keys):
    return lax.dot_general(
        q_rows, keys, (((1,), (1,)), ((), ())), preferred_element_type=jnp.float32
    )


def put_result(stage_ref, head, group, tile, positions, numer, total):
    result = (numer * (1.0 / total)).astype(stage_ref.dtype)
    stage_ref[tile * positions : (tile + 1) * positions, head * group : (head + 1) * group, :] = (
        result.reshape(positions, group, numer.shape[1])
    )


def out_copy(stage_ref, out_ref, sems, tile, positions):
    where = pl.ds(tile * positions, positions)
    return pltpu.make_async_copy(stage_ref.at[where], out_ref.at[where], sems.at[tile])


def first_kernel(axis, pair, kv_heads, factor, *refs):
    q_hbm, k_hbm, v_hbm = refs[:3]
    near_refs = refs[3 : 1 + 2 * pair]
    q_ref, top_ref, sums_ref = refs[1 + 2 * pair : 4 + 2 * pair]
    own_k, own_v, wide_ref, keys_ref, values_ref, kv_sems, q_sems = refs[4 + 2 * pair :]
    rows, heads, depth = q_ref.shape
    group = heads // kv_heads
    positions = tile_plan(rows, group)
    tile_rows = positions * group
    tiles = rows // positions
    me = lax.axis_index(axis)
    lane = lax.rem(me, pair)

    copy_k = pltpu.make_async_copy(k_hbm, own_k, kv_sems.at[0])
    copy_v = pltpu.make_async_copy(v_hbm, own_v, kv_sems.at[1])
    copy_q = pltpu.make_async_copy(q_hbm, q_ref, q_sems.at[0])
    copy_k.start()
    copy_v.start()
    copy_q.start()
    fill_ones(values_ref, depth)
    if pair > 1:
        split_into(near_refs[0][...], kv_heads, rows, wide_ref.at[0], keys_ref)
        split_into(near_refs[1][...], kv_heads, rows, wide_ref.at[1], values_ref)
    copy_k.wait()
    split_into(own_k[...], kv_heads, 0, wide_ref.at[2], keys_ref)
    copy_v.wait()
    split_into(own_v[...], kv_heads, 0, wide_ref.at[3], values_ref)
    copy_q.wait()
    bias = jnp.where(lane > 0, 0.0, NEG).astype(jnp.float32)

    for tile in range(tiles):
        for head in range(kv_heads):
            where = slice(tile * tile_rows, (tile + 1) * tile_rows)
            q_rows = tile_queries(q_ref, head, group, tile, positions)
            scores = scores_of(q_rows, keys_ref[head])
            own = scores[:, :rows].reshape(positions, group, rows)
            place = tile * positions + lax.broadcasted_iota(jnp.int32, own.shape, 0)
            own = jnp.where(lax.broadcasted_iota(jnp.int32, own.shape, 2) <= place, own, NEG)
            own = own.reshape(tile_rows, rows)
            if pair > 1:
                scores = jnp.concatenate([own, scores[:, rows:] + bias], axis=1)
            else:
                scores = own
            top = jnp.max(scores, axis=1, keepdims=True)
            weights = jnp.exp2((scores - top) * factor).astype(values_ref.dtype)
            top_ref[head, where, :] = jnp.broadcast_to(top, (tile_rows, depth))
            sums_ref[head, where, :] = jnp.dot(
                weights, values_ref[head], preferred_element_type=jnp.float32
            )


def keys_kernel(axis, pair, kv_heads, factor, hop, last, *refs):
    q_ref = refs[0]
    key_refs = refs[1 : 1 + pair]
    old_ref, sums_ref = refs[1 + pair : 3 + pair]
    held = hop > 1
    weights_ref, drop_ref, out_ref = refs[3 + held + pair : 6 + held + pair]
    top_ref = None if last else refs[6 + held + pair]
    wide_ref, keys_ref, stage_ref, out_sems = refs[-4:]
    rows, heads, depth = q_ref.shape
    group = heads // kv_heads
    positions = tile_plan(rows, group)
    tile_rows = positions * group
    tiles = rows // positions
    chip = lax.div(lax.axis_index(axis), pair)

    @pl.when(chip >= hop)
    def _():
        for block in range(pair):
            split_into(key_refs[block][...], kv_heads, block * rows, wide_ref.at[block], keys_ref)
        for tile in range(tiles):
            where = slice(tile * tile_rows, (tile + 1) * tile_rows)
            for head in range(kv_heads):
                q_rows = tile_queries(q_ref, head, group, tile, positions)
                scores = scores_of(q_rows, keys_ref[head])
                old = old_ref[head, where, :]
                top = jnp.maximum(jnp.max(scores, axis=1, keepdims=True), old)
                if top_ref is not None:
                    top_ref[head, where, :] = top
                drop_ref[head, where, :] = (old - top) * factor
                for part in range(pair * rows // depth):
                    weights_ref[head, part, where, :] = jnp.exp2(
                        (scores[:, part * depth : (part + 1) * depth] - top) * factor
                    ).astype(weights_ref.dtype)

    @pl.when(chip == hop - 1)
    def _():
        for tile in range(tiles):
            where = slice(tile * tile_rows, (tile + 1) * tile_rows)
            for head in range(kv_heads):
                put_result(
                    stage_ref, head, group, tile, positions,
                    sums_ref[head, where, :depth], sums_ref[head, where, depth:],
                )
            out_copy(stage_ref, out_ref, out_sems, tile, positions).start()
        for tile in range(tiles):
            out_copy(stage_ref, out_ref, out_sems, tile, positions).wait()


def values_kernel(axis, pair, kv_heads, hop, last, *refs):
    value_refs = refs[:pair]
    weights_ref, drop_ref, old_ref = refs[pair : 3 + pair]
    sums_ref, out_ref = refs[4 + pair : 6 + pair]
    wide_ref, values_ref, stage_ref, out_sems = refs[6 + pair :]
    rows, heads, depth = stage_ref.shape
    group = heads // kv_heads
    positions = tile_plan(rows, group)
    tile_rows = positions * group
    tiles = rows // positions
    chip = lax.div(lax.axis_index(axis), pair)

    def merged(head, tile):
        where = slice(tile * tile_rows, (tile + 1) * tile_rows)
        weights = jnp.concatenate(
            [weights_ref[head, part, where, :] for part in range(pair * rows // depth)], axis=1
        )
        sums = jnp.dot(weights, values_ref[head], preferred_element_type=jnp.float32)
        rescale = jnp.exp2(drop_ref[head, where, :])
        return (
            old_ref[head, where, :depth] * rescale + sums[:, :depth],
            old_ref[head, where, depth:] * rescale + sums[:, depth:],
        )

    @pl.when(chip >= hop)
    def _():
        fill_ones(values_ref, depth)
        for block in range(pair):
            split_into(value_refs[block][...], kv_heads, block * rows, wide_ref.at[block], values_ref)
        for tile in range(tiles):
            where = slice(tile * tile_rows, (tile + 1) * tile_rows)
            for head in range(kv_heads):
                numer, total = merged(head, tile)
                if last:
                    put_result(stage_ref, head, group, tile, positions, numer, total)
                else:
                    sums_ref[head, where, :depth] = numer
                    sums_ref[head, where, depth:] = total
            if last:
                out_copy(stage_ref, out_ref, out_sems, tile, positions).start()
        if last:
            for tile in range(tiles):
                out_copy(stage_ref, out_ref, out_sems, tile, positions).wait()


def in_vmem(array):
    return pltpu.with_memory_space_constraint(array, pltpu.VMEM)


def in_hbm(array):
    return pltpu.with_memory_space_constraint(array, pltpu.HBM)


def local(ctx_size, queries, keys, values):
    rows, heads, depth = queries.shape
    kv_heads = keys.shape[1]
    group = heads // kv_heads
    pair = 2 if ctx_size % 2 == 0 else 1
    chips = ctx_size // pair
    factor = math.log2(math.e) / math.sqrt(depth)
    vmem = pl.BlockSpec(memory_space=pltpu.VMEM)
    anywhere = pl.BlockSpec(memory_space=pl.ANY)

    keys = keys.reshape(rows * kv_heads, depth)
    values = values.reshape(rows * kv_heads, depth)
    swap = [(i, i ^ 1) for i in range(ctx_size)]

    def across(array, hop, cross):
        route = [
            (i, (i // pair + hop) % chips * pair + (i % pair ^ cross)) for i in range(ctx_size)
        ]
        return lax.ppermute(array, "ctx", route)

    def far_pair(hop):
        far_keys = [across(keys, hop, pair - 1)]
        far_values = [across(values, hop, pair - 1)]
        if pair == 2 and DIRECT:
            far_values.append(across(values, hop, 0))
        return far_keys, far_values

    far = [far_pair(1)]
    near = []
    if pair == 2:
        near = [lax.ppermute(keys, "ctx", swap), lax.ppermute(values, "ctx", swap)]

    positions = tile_plan(rows, group)
    tiles = rows // positions
    work = heads * rows * rows * pair
    cost = pl.CostEstimate(
        flops=work * depth * 4, bytes_accessed=heads * rows * depth * 2, transcendentals=work
    )
    def wide_scratch(count):
        return pltpu.VMEM((count, *keys.shape), jnp.float32)

    keys_scratch = pltpu.VMEM((kv_heads, pair * rows, depth), keys.dtype)
    values_scratch = pltpu.VMEM((kv_heads, pair * rows, 2 * depth), keys.dtype)
    out_scratch = [pltpu.VMEM(queries.shape, queries.dtype), pltpu.SemaphoreType.DMA((tiles,))]
    params = pltpu.CompilerParams(vmem_limit_bytes=VMEM_LIMIT)
    out_shape = jax.ShapeDtypeStruct(queries.shape, queries.dtype)
    top_shape = pltpu.VMEM((kv_heads, rows * group, depth), jnp.float32)
    sums_shape = pltpu.VMEM((kv_heads, rows * group, 2 * depth), jnp.float32)
    weights_shape = pltpu.VMEM(
        (kv_heads, pair * rows // depth, rows * group, depth), values.dtype
    )
    q_vmem, top, sums = pl.pallas_call(
        functools.partial(first_kernel, "ctx", pair, kv_heads, factor),
        out_shape=(pltpu.VMEM(queries.shape, queries.dtype), top_shape, sums_shape),
        in_specs=[anywhere] * 3 + [vmem] * len(near),
        out_specs=(vmem,) * 3,
        scratch_shapes=[
            pltpu.VMEM(keys.shape, keys.dtype),
            pltpu.VMEM(keys.shape, keys.dtype),
            wide_scratch(2 * pair),
            keys_scratch,
            values_scratch,
            pltpu.SemaphoreType.DMA((2,)),
            pltpu.SemaphoreType.DMA((1,)),
        ],
        compiler_params=params,
        cost_estimate=cost,
    )(*[in_hbm(x) for x in (queries, keys, values)], *[in_vmem(x) for x in near])

    out = None
    for hop in range(1, chips):
        last = hop == chips - 1
        if not last:
            far.append(far_pair(hop + 1))
        all_keys, all_values = far[hop - 1]
        first_keys, top = lax.optimization_barrier((all_keys[0], top))
        all_keys = [first_keys]
        if pair == 2:
            all_keys.append(lax.ppermute(first_keys, "ctx", swap))
            if not DIRECT:
                all_keys[1], first_values = lax.optimization_barrier((all_keys[1], all_values[0]))
                all_values = [first_values, lax.ppermute(first_values, "ctx", swap)]
        held = [] if out is None else [in_hbm(out)]
        weights, drop, out, *new_top = pl.pallas_call(
            functools.partial(keys_kernel, "ctx", pair, kv_heads, factor, hop, last),
            out_shape=(weights_shape, top_shape, out_shape) + (() if last else (top_shape,)),
            in_specs=[vmem] * (3 + pair) + [anywhere] * len(held),
            out_specs=(vmem, vmem, anywhere) + (() if last else (vmem,)),
            scratch_shapes=[wide_scratch(pair), keys_scratch, *out_scratch],
            input_output_aliases={3 + pair: 2} if held else {},
            compiler_params=params,
            cost_estimate=cost,
        )(
            in_vmem(q_vmem),
            *[in_vmem(x) for x in all_keys],
            in_vmem(top),
            in_vmem(sums),
            *held,
        )
        top = top if last else new_top[0]
        sums, out = pl.pallas_call(
            functools.partial(values_kernel, "ctx", pair, kv_heads, hop, last),
            out_shape=(sums_shape, out_shape),
            in_specs=[vmem] * (3 + pair) + [anywhere],
            out_specs=(vmem, anywhere),
            scratch_shapes=[wide_scratch(pair), values_scratch, *out_scratch],
            input_output_aliases={2 + pair: 0, 3 + pair: 1},
            compiler_params=params,
            cost_estimate=cost,
        )(
            *[in_vmem(x) for x in all_values],
            *[in_vmem(x) for x in (weights, drop, sums)],
            in_hbm(out),
        )
    return out


def solution(mesh):
    return jax.shard_map(
        functools.partial(local, mesh.shape["ctx"]),
        mesh=mesh,
        in_specs=(
            P(("seq", "ctx"), "head", None),
            P(("seq", "ctx"), "head", None),
            P(("seq", "ctx"), "head", None),
        ),
        out_specs=P(("seq", "ctx"), "head", None),
        check_vma=False,
    )
```

time: 11 us -> 10 us (0.909)
  waiting for transfers between devices: 2.38 us -> 1.39 us
    ppermute x4, waiting for transfers between devices: 2.38 us -> 1.38 us  [the longest x2 1.16 us: across(): return lax.ppermute(array, 'ctx', route)]
    pallas_call x1 -> x2, Pallas kernels: 2.63 us -> 2.79 us  [the longest x1 1.63 us: local(): pl.pallas_call(functools.partial(values_kernel, 'ctx', pair, kv_heads, ho...]
    pallas_call x1, Pallas kernels: 2.93 us -> 2.78 us  [local(): pl.pallas_call(functools.partial(first_kernel, 'ctx', pair, kv_heads, fac...]
  transfers between devices with their start and end apart: 6 -> 6, of which waited for: 4 -> 3; matrix products, arithmetic and copies ran while one was open for 0% -> 0% of each run, Pallas kernels for 27% -> 40%
where the time goes in v2:
time: 10 us; the launch traced here: 9.87 us
  Pallas kernels  5.58 us (56%)
  starting transfers between devices  2.88 us (29%)
  waiting for transfers between devices  1.39 us (14%)
    pallas_call x1, Pallas kernels, local(): pl.pallas_call(functools.partial(first_kernel, 'ctx', pair, kv_heads, fac...  2.78 us
    ppermute x2, starting transfers between devices, across(): return lax.ppermute(array, 'ctx', route)  1.75 us
    pallas_call x1, Pallas kernels, local(): pl.pallas_call(functools.partial(values_kernel, 'ctx', pair, kv_heads, ho...  1.63 us
    pallas_call x1, Pallas kernels, local(): pl.pallas_call(functools.partial(keys_kernel, 'ctx', pair, kv_heads, fact...  1.17 us
    ppermute x2, waiting for transfers between devices, across(): return lax.ppermute(array, 'ctx', route)  1.16 us
    ppermute x2, starting transfers between devices, local(): near = [lax.ppermute(keys, 'ctx', swap), lax.ppermute(values, 'ctx', swap)]  0.68 us
    ppermute x1, starting transfers between devices, local(): all_keys.append(lax.ppermute(first_keys, 'ctx', swap))  0.23 us
    ppermute x1, starting transfers between devices, local(): all_values = [first_values, lax.ppermute(first_values, 'ctx', swap)]  0.23 us
  transfers between devices with their start and end apart: 6, of which 3 were waited for; matrix products, arithmetic and copies ran while one was open for 0% of the time, Pallas kernels for 40%

profile of v2, /device:TPU:7, one launch (start us, length us, event | category | flops | bytes accessed | tf_op | source)
XLA Modules:
  0.0 9.9 jit_solution(3918773420481809594)
XLA Ops:
  0.0 0.7 %collective-permute-start.1 = (bf16[256,128]{1,0:T(8,128)(2,1)}, bf16[256,128]{1,0:T(8,128)(2,1)S(1)}, u32[]{:S(2)}, u32[]{:S(2)}) collective-permute-start(bf16[256,128]{1,0:T(8,128)(2,1)} %bitcast.2), channel_id=1, source_target_pairs={{0,8},{8,0},{16,24},{24,16},{1,9},{9,1},{17,25},{25,17},{2,10},{10... | collective-permute-start | bytes 196616 | tf_op jit(solution)/shard_map/ppermute | solution.py:243
  0.7 0.0 collective-permute-start.2
  0.7 0.6 %collective-permute-start = (bf16[256,128]{1,0:T(8,128)(2,1)}, bf16[256,128]{1,0:T(8,128)(2,1)S(1)}, u32[]{:S(2)}, u32[]{:S(2)}) collective-permute-start(bf16[256,128]{1,0:T(8,128)(2,1)} %bitcast.3), channel_id=1, source_target_pairs={{0,24},{8,16},{16,8},{24,0},{1,25},{9,17},{17,9},{25,1},{2,26},{10... | collective-permute-start | bytes 196616 | tf_op jit(solution)/shard_map/ppermute | solution.py:231
  1.3 1.1 %collective-permute-start.4 = (bf16[256,128]{1,0:T(8,128)(2,1)}, bf16[256,128]{1,0:T(8,128)(2,1)S(1)}, u32[]{:S(2)}, u32[]{:S(2)}) collective-permute-start(bf16[256,128]{1,0:T(8,128)(2,1)} %bitcast.6), channel_id=1, source_target_pairs={{0,24},{8,16},{16,8},{24,0},{1,25},{9,17},{17,9},{25,1},{2,26},{10... | collective-permute-start | bytes 196616 | tf_op jit(solution)/shard_map/ppermute | solution.py:231
  2.4 0.0 collective-permute-done.1.refs_3_
  2.4 0.0 collective-permute-done.2.refs_4_
  2.4 2.8 %shard_map.37 = (bf16[128,32,128]{2,1,0:T(8,128)(2,1)S(1)}, f32[2,2048,128]{2,1,0:T(8,128)S(1)}, f32[2,2048,256]{2,1,0:T(8,128)S(1)}) custom-call(bf16[128,32,128]{2,1,0:T(8,128)(2,1)} %refs_0_.1, bf16[256,128]{1,0:T(8,128)(2,1)} %bitcast.4, bf16[256,128]{1,0:T(8,128)(2,1)} %bitcast.7, bf16[256,128]{1,0:T(8,128)(2,1)S(1)} %collective-permute-done.1.refs_3_, ...), custom_call_target="tpu_custom_call" | custom-call | flops 536870912 | bytes 1048576 | tf_op jit(solution)/shard_map/pallas_call | solution.py:264
  5.2 0.4 %collective-permute-done.refs_1_ = bf16[256,128]{1,0:T(8,128)(2,1)S(1)} collective-permute-done((bf16[256,128]{1,0:T(8,128)(2,1)}, bf16[256,128]{1,0:T(8,128)(2,1)S(1)}, u32[]{:S(2)}, u32[]{:S(2)}) %collective-permute-start) | collective-permute-done | bytes 65568 | tf_op jit(solution)/shard_map/ppermute | solution.py:231
  5.6 0.2 %collective-permute-start.3 = (bf16[256,128]{1,0:T(8,128)(2,1)S(1)}, bf16[256,128]{1,0:T(8,128)(2,1)S(1)}, u32[]{:S(2)}, u32[]{:S(2)}) collective-permute-start(bf16[256,128]{1,0:T(8,128)(2,1)S(1)} %collective-permute-done.refs_1_), channel_id=1, source_target_pairs={{0,8},{8,0},{16,24},{24,16},{1,9},{9,1},{17,25},{25,17},{2,10},{10... | collective-permute-start | bytes 196616 | tf_op jit(solution)/shard_map/ppermute | solution.py:291
  5.8 0.8 %collective-permute-done.4.refs_0_ = bf16[256,128]{1,0:T(8,128)(2,1)S(1)} collective-permute-done((bf16[256,128]{1,0:T(8,128)(2,1)}, bf16[256,128]{1,0:T(8,128)(2,1)S(1)}, u32[]{:S(2)}, u32[]{:S(2)}) %collective-permute-start.4) | collective-permute-done | bytes 65568 | tf_op jit(solution)/shard_map/ppermute | solution.py:231
  6.6 0.2 %collective-permute-done.3.refs_2_ = bf16[256,128]{1,0:T(8,128)(2,1)S(1)} collective-permute-done((bf16[256,128]{1,0:T(8,128)(2,1)S(1)}, bf16[256,128]{1,0:T(8,128)(2,1)S(1)}, u32[]{:S(2)}, u32[]{:S(2)}) %collective-permute-start.3) | collective-permute-done | bytes 65568 | tf_op jit(solution)/shard_map/ppermute | solution.py:291
  6.8 0.2 %collective-permute-start.5 = (bf16[256,128]{1,0:T(8,128)(2,1)S(1)}, bf16[256,128]{1,0:T(8,128)(2,1)S(1)}, u32[]{:S(2)}, u32[]{:S(2)}) collective-permute-start(bf16[256,128]{1,0:T(8,128)(2,1)S(1)} %collective-permute-done.4.refs_0_), channel_id=1, source_target_pairs={{0,8},{8,0},{16,24},{24,16},{1,9},{9,1},{17,25},{25,17},{2,10},{10... | collective-permute-start | bytes 196616 | tf_op jit(solution)/shard_map/ppermute | solution.py:294
  7.1 1.2 %shard_map.38 = (bf16[2,2,2048,128]{3,2,1,0:T(8,128)(2,1)S(1)}, f32[2,2048,128]{2,1,0:T(8,128)S(1)}, bf16[128,32,128]{2,1,0:T(8,128)(2,1)}) custom-call(bf16[128,32,128]{2,1,0:T(8,128)(2,1)S(1)} %get-tuple-element.19.refs_0_, bf16[256,128]{1,0:T(8,128)(2,1)S(1)} %collective-permute-done.refs_1_, bf16[256,128]{1,0:T(8,128)(2,1)S(1)} %collective-permute-done.3.refs_2_, ...), custom_call_target="tpu_custom_call" | custom-call | flops 536870912 | bytes 1048576 | tf_op jit(solution)/shard_map/pallas_call | solution.py:296
  8.2 0.0 collective-permute-done.5.refs_1_
  8.2 1.6 %shard_map.39 = (f32[2,2048,256]{2,1,0:T(8,128)S(1)}, bf16[128,32,128]{2,1,0:T(8,128)(2,1)}) custom-call(bf16[256,128]{1,0:T(8,128)(2,1)S(1)} %collective-permute-done.4.refs_0_, bf16[256,128]{1,0:T(8,128)(2,1)S(1)} %collective-permute-done.5.refs_1_, ...), custom_call_target="tpu_custom_call", output_to_operand_aliasing={{0}: (4, {}), {1}: (5, {})} | custom-call | flops 536870912 | bytes 1048576 | tf_op jit(solution)/shard_map/pallas_call | solution.py:313
Async XLA Ops:
  0.0 2.4 %collective-permute-start.1 = (bf16[256,128]{1,0:T(8,128)(2,1)}, bf16[256,128]{1,0:T(8,128)(2,1)S(1)}, u32[]{:S(2)}, u32[]{:S(2)}) collective-permute-start(bf16[256,128]{1,0:T(8,128)(2,1)} %bitcast.2), channel_id=1, source_target_pairs={{0,8},{8,0},{16,24},{24,16},{1,9},{9,1},{17,25},{25,17},{2,10},{10... | collective-permute-start | bytes 196616 | tf_op jit(solution)/shard_map/ppermute | solution.py:243
  0.7 1.8 %collective-permute-start.2 = (bf16[256,128]{1,0:T(8,128)(2,1)}, bf16[256,128]{1,0:T(8,128)(2,1)S(1)}, u32[]{:S(2)}, u32[]{:S(2)}) collective-permute-start(bf16[256,128]{1,0:T(8,128)(2,1)} %bitcast.5), channel_id=1, source_target_pairs={{0,8},{8,0},{16,24},{24,16},{1,9},{9,1},{17,25},{25,17},{2,10},{10... | collective-permute-start | bytes 196616 | tf_op jit(solution)/shard_map/ppermute | solution.py:243
  0.7 4.9 %collective-permute-start = (bf16[256,128]{1,0:T(8,128)(2,1)}, bf16[256,128]{1,0:T(8,128)(2,1)S(1)}, u32[]{:S(2)}, u32[]{:S(2)}) collective-permute-start(bf16[256,128]{1,0:T(8,128)(2,1)} %bitcast.3), channel_id=1, source_target_pairs={{0,24},{8,16},{16,8},{24,0},{1,25},{9,17},{17,9},{25,1},{2,26},{10... | collective-permute-start | bytes 196616 | tf_op jit(solution)/shard_map/ppermute | solution.py:231
  1.3 5.3 %collective-permute-start.4 = (bf16[256,128]{1,0:T(8,128)(2,1)}, bf16[256,128]{1,0:T(8,128)(2,1)S(1)}, u32[]{:S(2)}, u32[]{:S(2)}) collective-permute-start(bf16[256,128]{1,0:T(8,128)(2,1)} %bitcast.6), channel_id=1, source_target_pairs={{0,24},{8,16},{16,8},{24,0},{1,25},{9,17},{17,9},{25,1},{2,26},{10... | collective-permute-start | bytes 196616 | tf_op jit(solution)/shard_map/ppermute | solution.py:231
  5.6 1.3 %collective-permute-start.3 = (bf16[256,128]{1,0:T(8,128)(2,1)S(1)}, bf16[256,128]{1,0:T(8,128)(2,1)S(1)}, u32[]{:S(2)}, u32[]{:S(2)}) collective-permute-start(bf16[256,128]{1,0:T(8,128)(2,1)S(1)} %collective-permute-done.refs_1_), channel_id=1, source_target_pairs={{0,8},{8,0},{16,24},{24,16},{1,9},{9,1},{17,25},{25,17},{2,10},{10... | collective-permute-start | bytes 196616 | tf_op jit(solution)/shard_map/ppermute | solution.py:291
  6.8 1.4 %collective-permute-start.5 = (bf16[256,128]{1,0:T(8,128)(2,1)S(1)}, bf16[256,128]{1,0:T(8,128)(2,1)S(1)}, u32[]{:S(2)}, u32[]{:S(2)}) collective-permute-start(bf16[256,128]{1,0:T(8,128)(2,1)S(1)} %collective-permute-done.4.refs_0_), channel_id=1, source_target_pairs={{0,8},{8,0},{16,24},{24,16},{1,9},{9,1},{17,25},{25,17},{2,10},{10... | collective-permute-start | bytes 196616 | tf_op jit(solution)/shard_map/ppermute | solution.py:294

commit v3 on v2

--- a/solution.py
+++ b/solution.py
@@ -9,7 +9,7 @@
 from jax.sharding import PartitionSpec as P
 
 VMEM_LIMIT = 30 * 1024 * 1024
-TILE_ROWS = 256
+TILE_ROWS = 512
 NEG = -1e30
 DIRECT = False
 
@@ -58,34 +58,39 @@
     return pltpu.make_async_copy(stage_ref.at[where], out_ref.at[where], sems.at[tile])
 
 
+def load_kernel(kv_heads, *refs):
+    k_hbm, v_hbm, keys_ref, values_ref, own_k, own_v, wide_ref, sems = refs
+    copies = [
+        pltpu.make_async_copy(source, target, sems.at[i])
+        for i, (source, target) in enumerate(((k_hbm, own_k), (v_hbm, own_v)))
+    ]
+    for copy in copies:
+        copy.start()
+    fill_ones(values_ref, keys_ref.shape[2])
+    copies[0].wait()
+    split_into(own_k[...], kv_heads, 0, wide_ref.at[0], keys_ref)
+    copies[1].wait()
+    split_into(own_v[...], kv_heads, 0, wide_ref.at[1], values_ref)
+
+
 def first_kernel(axis, pair, kv_heads, factor, *refs):
-    q_hbm, k_hbm, v_hbm = refs[:3]
+    q_ref, own_keys_ref, own_values_ref = refs[:3]
     near_refs = refs[3 : 1 + 2 * pair]
-    q_ref, top_ref, sums_ref = refs[1 + 2 * pair : 4 + 2 * pair]
-    own_k, own_v, wide_ref, keys_ref, values_ref, kv_sems, q_sems = refs[4 + 2 * pair :]
+    top_ref, sums_ref = refs[1 + 2 * pair : 3 + 2 * pair]
+    wide_ref, keys_ref, values_ref = refs[3 + 2 * pair :]
     rows, heads, depth = q_ref.shape
     group = heads // kv_heads
     positions = tile_plan(rows, group)
     tile_rows = positions * group
     tiles = rows // positions
-    me = lax.axis_index(axis)
-    lane = lax.rem(me, pair)
-
-    copy_k = pltpu.make_async_copy(k_hbm, own_k, kv_sems.at[0])
-    copy_v = pltpu.make_async_copy(v_hbm, own_v, kv_sems.at[1])
-    copy_q = pltpu.make_async_copy(q_hbm, q_ref, q_sems.at[0])
-    copy_k.start()
-    copy_v.start()
-    copy_q.start()
-    fill_ones(values_ref, depth)
+    lane = lax.rem(lax.axis_index(axis), pair)
+
+    keys_ref[:, :rows, :] = own_keys_ref[...]
+    values_ref[:, :rows, :] = own_values_ref[...]
     if pair > 1:
+        fill_ones(values_ref.at[:, rows:], depth)
         split_into(near_refs[0][...], kv_heads, rows, wide_ref.at[0], keys_ref)
         split_into(near_refs[1][...], kv_heads, rows, wide_ref.at[1], values_ref)
-    copy_k.wait()
-    split_into(own_k[...], kv_heads, 0, wide_ref.at[2], keys_ref)
-    copy_v.wait()
-    split_into(own_v[...], kv_heads, 0, wide_ref.at[3], values_ref)
-    copy_q.wait()
     bias = jnp.where(lane > 0, 0.0, NEG).astype(jnp.float32)
 
     for tile in range(tiles):
@@ -220,6 +225,7 @@
     vmem = pl.BlockSpec(memory_space=pltpu.VMEM)
     anywhere = pl.BlockSpec(memory_space=pl.ANY)
 
+    raw_keys, raw_values = keys, values
     keys = keys.reshape(rows * kv_heads, depth)
     values = values.reshape(rows * kv_heads, depth)
     swap = [(i, i ^ 1) for i in range(ctx_size)]
@@ -228,10 +234,10 @@
         route = [
             (i, (i // pair + hop) % chips * pair + (i % pair ^ cross)) for i in range(ctx_size)
         ]
-        return lax.ppermute(array, "ctx", route)
+        return lax.ppermute(array, "ctx", route).reshape(rows * kv_heads, depth)
 
     def far_pair(hop):
-        far_keys = [across(keys, hop, pair - 1)]
+        far_keys = [across(raw_keys, hop, pair - 1)]
         far_values = [across(values, hop, pair - 1)]
         if pair == 2 and DIRECT:
             far_values.append(across(values, hop, 0))
@@ -240,7 +246,8 @@
     far = [far_pair(1)]
     near = []
     if pair == 2:
-        near = [lax.ppermute(keys, "ctx", swap), lax.ppermute(values, "ctx", swap)]
+        near_values = lax.ppermute(raw_values, "ctx", swap).reshape(rows * kv_heads, depth)
+        near = [lax.ppermute(keys, "ctx", swap), near_values]
 
     positions = tile_plan(rows, group)
     tiles = rows // positions
@@ -261,23 +268,33 @@
     weights_shape = pltpu.VMEM(
         (kv_heads, pair * rows // depth, rows * group, depth), values.dtype
     )
-    q_vmem, top, sums = pl.pallas_call(
-        functools.partial(first_kernel, "ctx", pair, kv_heads, factor),
-        out_shape=(pltpu.VMEM(queries.shape, queries.dtype), top_shape, sums_shape),
-        in_specs=[anywhere] * 3 + [vmem] * len(near),
-        out_specs=(vmem,) * 3,
+    q_vmem = queries
+    own_keys, own_values = pl.pallas_call(
+        functools.partial(load_kernel, kv_heads),
+        out_shape=(
+            pltpu.VMEM((kv_heads, rows, depth), keys.dtype),
+            pltpu.VMEM((kv_heads, rows, 2 * depth), values.dtype),
+        ),
+        in_specs=[anywhere] * 2,
+        out_specs=(vmem,) * 2,
         scratch_shapes=[
             pltpu.VMEM(keys.shape, keys.dtype),
-            pltpu.VMEM(keys.shape, keys.dtype),
-            wide_scratch(2 * pair),
-            keys_scratch,
-            values_scratch,
+            pltpu.VMEM(values.shape, values.dtype),
+            wide_scratch(2),
             pltpu.SemaphoreType.DMA((2,)),
-            pltpu.SemaphoreType.DMA((1,)),
         ],
         compiler_params=params,
-        cost_estimate=cost,
-    )(*[in_hbm(x) for x in (queries, keys, values)], *[in_vmem(x) for x in near])
+        cost_estimate=pl.CostEstimate(flops=work * depth * 400, bytes_accessed=heads * rows * depth * 200, transcendentals=work),
+    )(*[in_hbm(x) for x in (keys, values)])
+    top, sums = pl.pallas_call(
+        functools.partial(first_kernel, "ctx", pair, kv_heads, factor),
+        out_shape=(top_shape, sums_shape),
+        in_specs=[vmem] * (3 + len(near)),
+        out_specs=(vmem,) * 2,
+        scratch_shapes=[wide_scratch(2), keys_scratch, values_scratch],
+        compiler_params=params,
+        cost_estimate=pl.CostEstimate(flops=work * depth * 400, bytes_accessed=heads * rows * depth * 200, transcendentals=work),
+    )(*[in_vmem(x) for x in (q_vmem, own_keys, own_values, *near)])
 
     out = None
     for hop in range(1, chips):

time: 10 us -> 9.59 us (0.959)
  Pallas kernels: 5.58 us -> 5.11 us
  waiting for transfers between devices: 1.39 us -> 0.93 us
  starting transfers between devices: 2.88 us -> 3.33 us
    pallas_call x1, Pallas kernels: 2.78 us -> 1.49 us  [local(): pl.pallas_call(functools.partial(first_kernel, 'ctx', pair, kv_heads, fac...]
    pallas_call x0 -> x1, Pallas kernels: none -> 0.91 us  [local(): pl.pallas_call(functools.partial(load_kernel, kv_heads), out_shape=(pltpu...]
    ppermute x1, starting transfers between devices: 0.23 us -> 0.56 us  [local(): all_keys.append(lax.ppermute(first_keys, 'ctx', swap))]
    ppermute x4, waiting for transfers between devices: 1.17 us -> 0.85 us  [the longest x2 0.84 us: across(): return lax.ppermute(array, 'ctx', route).reshape(rows * kv_heads, depth)]
    ppermute x1, waiting for transfers between devices: 0.22 us -> 0.08 us  [local(): all_keys.append(lax.ppermute(first_keys, 'ctx', swap))]
    ppermute x1, starting transfers between devices: 0.23 us -> 0.35 us  [local(): all_values = [first_values, lax.ppermute(first_values, 'ctx', swap)]]
  transfers between devices with their start and end apart: 6 -> 6, of which waited for: 3 -> 2; matrix products, arithmetic and copies ran while one was open for 0% -> 0% of each run, Pallas kernels for 40% -> 38%
where the time goes in v3:
time: 9.59 us; the launch traced here: 9.44 us
  Pallas kernels  5.11 us (53%)
  starting transfers between devices  3.33 us (35%)
  waiting for transfers between devices  0.93 us (10%)
    ppermute x2, starting transfers between devices, across(): return lax.ppermute(array, 'ctx', route).reshape(rows * kv_heads, depth)  1.91 us
    pallas_call x1, Pallas kernels, local(): pl.pallas_call(functools.partial(values_kernel, 'ctx', pair, kv_heads, ho...  1.58 us
    pallas_call x1, Pallas kernels, local(): pl.pallas_call(functools.partial(first_kernel, 'ctx', pair, kv_heads, fac...  1.49 us
    pallas_call x1, Pallas kernels, local(): pl.pallas_call(functools.partial(keys_kernel, 'ctx', pair, kv_heads, fact...  1.13 us
    pallas_call x1, Pallas kernels, local(): pl.pallas_call(functools.partial(load_kernel, kv_heads), out_shape=(pltpu...  0.91 us
    ppermute x2, waiting for transfers between devices, across(): return lax.ppermute(array, 'ctx', route).reshape(rows * kv_heads, depth)  0.84 us
    ppermute x1, starting transfers between devices, local(): all_keys.append(lax.ppermute(first_keys, 'ctx', swap))  0.56 us
    ppermute x1, starting transfers between devices, local(): lax.ppermute(raw_values, 'ctx', swap).reshape(rows * kv_heads, depth)  0.51 us
  transfers between devices with their start and end apart: 6, of which 2 were waited for; matrix products, arithmetic and copies ran while one was open for 0% of the time, Pallas kernels for 38%

profile of v3, /device:TPU:7, one launch (start us, length us, event | category | flops | bytes accessed | tf_op | source)
XLA Modules:
  0.0 9.4 jit_solution(1803644720445409458)
XLA Ops:
  0.0 0.8 %collective-permute-start = (bf16[128,2,128]{2,1,0:T(2,128)(2,1)}, bf16[128,2,128]{2,1,0:T(2,128)(2,1)S(1)}, u32[]{:S(2)}, u32[]{:S(2)}) collective-permute-start(bf16[128,2,128]{2,1,0:T(2,128)(2,1)} %param.4), channel_id=1, source_target_pairs={{0,24},{8,16},{16,8},{24,0},{1,25},{9,17},{17,9},{25,1},{2,26},{10... | collective-permute-start | bytes 196616 | tf_op jit(solution)/shard_map/ppermute | solution.py:237
  0.8 0.0 collective-permute-start.1
  0.8 0.5 %collective-permute-start.2 = (bf16[128,2,128]{2,1,0:T(2,128)(2,1)}, bf16[128,2,128]{2,1,0:T(2,128)(2,1)S(1)}, u32[]{:S(2)}, u32[]{:S(2)}) collective-permute-start(bf16[128,2,128]{2,1,0:T(2,128)(2,1)} %param.5), channel_id=1, source_target_pairs={{0,8},{8,0},{16,24},{24,16},{1,9},{9,1},{17,25},{25,17},{2,10},{10... | collective-permute-start | bytes 196616 | tf_op jit(solution)/shard_map/ppermute | solution.py:249
  1.3 0.0 copy-start
  1.3 1.1 %collective-permute-start.4 = (bf16[256,128]{1,0:T(8,128)(2,1)}, bf16[256,128]{1,0:T(8,128)(2,1)S(1)}, u32[]{:S(2)}, u32[]{:S(2)}) collective-permute-start(bf16[256,128]{1,0:T(8,128)(2,1)} %bitcast.9), channel_id=1, source_target_pairs={{0,24},{8,16},{16,8},{24,0},{1,25},{9,17},{17,9},{25,1},{2,26},{10... | collective-permute-start | bytes 196616 | tf_op jit(solution)/shard_map/ppermute | solution.py:237
  2.4 0.9 %shard_map.37 = (bf16[2,128,128]{2,1,0:T(8,128)(2,1)S(1)}, bf16[2,128,256]{2,1,0:T(8,128)(2,1)S(1)}) custom-call(bf16[256,128]{1,0:T(8,128)(2,1)} %bitcast.8, bf16[256,128]{1,0:T(8,128)(2,1)} %bitcast.10), custom_call_target="tpu_custom_call" | custom-call | flops 53687091200 | bytes 104857600 | tf_op jit(solution)/shard_map/pallas_call | solution.py:272
  3.4 0.0 collective-permute-done.1.refs_3_
  3.4 0.0 collective-permute-done.2
  3.4 0.0 copy-done
  3.4 1.5 %shard_map.38 = (f32[2,2048,128]{2,1,0:T(8,128)S(1)}, f32[2,2048,256]{2,1,0:T(8,128)S(1)}) custom-call(bf16[128,32,128]{2,1,0:T(8,128)(2,1)S(1)} %copy-done, bf16[2,128,128]{2,1,0:T(8,128)(2,1)S(1)} %get-tuple-element.17.refs_1_, bf16[2,128,256]{2,1,0:T(8,128)(2,1)S(1)} %get-tuple-element.18.refs_2_, bf16[256,128]{1,0:T(8,128)(2,1)S(1)} %collective-permute-done.1.refs_3_, ...), custom_call_target="tpu_custom_call" | custom-call | flops 53687091200 | bytes 104857600 | tf_op jit(solution)/shard_map/pallas_call | solution.py:289
  4.9 0.0 collective-permute-done
  4.9 0.6 %collective-permute-start.3 = (bf16[256,128]{1,0:T(8,128)(2,1)S(1)}, bf16[256,128]{1,0:T(8,128)(2,1)S(1)}, u32[]{:S(2)}, u32[]{:S(2)}) collective-permute-start(bf16[256,128]{1,0:T(8,128)(2,1)S(1)} %bitcast.4), channel_id=1, source_target_pairs={{0,8},{8,0},{16,24},{24,16},{1,9},{9,1},{17,25},{25,17},{2,10},{10... | collective-permute-start | bytes 196616 | tf_op jit(solution)/shard_map/ppermute | solution.py:308
  5.5 0.8 %collective-permute-done.4.refs_0_ = bf16[256,128]{1,0:T(8,128)(2,1)S(1)} collective-permute-done((bf16[256,128]{1,0:T(8,128)(2,1)}, bf16[256,128]{1,0:T(8,128)(2,1)S(1)}, u32[]{:S(2)}, u32[]{:S(2)}) %collective-permute-start.4) | collective-permute-done | bytes 65568 | tf_op jit(solution)/shard_map/ppermute | solution.py:237
  6.3 0.1 collective-permute-done.3.refs_2_
  6.4 0.4 %collective-permute-start.5 = (bf16[256,128]{1,0:T(8,128)(2,1)S(1)}, bf16[256,128]{1,0:T(8,128)(2,1)S(1)}, u32[]{:S(2)}, u32[]{:S(2)}) collective-permute-start(bf16[256,128]{1,0:T(8,128)(2,1)S(1)} %collective-permute-done.4.refs_0_), channel_id=1, source_target_pairs={{0,8},{8,0},{16,24},{24,16},{1,9},{9,1},{17,25},{25,17},{2,10},{10... | collective-permute-start | bytes 196616 | tf_op jit(solution)/shard_map/ppermute | solution.py:311
  6.7 1.1 %shard_map.39 = (bf16[2,2,2048,128]{3,2,1,0:T(8,128)(2,1)S(1)}, f32[2,2048,128]{2,1,0:T(8,128)S(1)}, bf16[128,32,128]{2,1,0:T(8,128)(2,1)}) custom-call(bf16[128,32,128]{2,1,0:T(8,128)(2,1)S(1)} %copy-done, bf16[256,128]{1,0:T(8,128)(2,1)S(1)} %bitcast.5, bf16[256,128]{1,0:T(8,128)(2,1)S(1)} %collective-permute-done.3.refs_2_, ...), custom_call_target="tpu_custom_call" | custom-call | flops 536870912 | bytes 1048576 | tf_op jit(solution)/shard_map/pallas_call | solution.py:313
  7.9 0.0 collective-permute-done.5.refs_1_
  7.9 1.6 %shard_map.40 = (f32[2,2048,256]{2,1,0:T(8,128)S(1)}, bf16[128,32,128]{2,1,0:T(8,128)(2,1)}) custom-call(bf16[256,128]{1,0:T(8,128)(2,1)S(1)} %collective-permute-done.4.refs_0_, bf16[256,128]{1,0:T(8,128)(2,1)S(1)} %collective-permute-done.5.refs_1_, ...), custom_call_target="tpu_custom_call", output_to_operand_aliasing={{0}: (4, {}), {1}: (5, {})} | custom-call | flops 536870912 | bytes 1048576 | tf_op jit(solution)/shard_map/pallas_call | solution.py:330
Async XLA Ops:
  0.0 4.9 %collective-permute-start = (bf16[128,2,128]{2,1,0:T(2,128)(2,1)}, bf16[128,2,128]{2,1,0:T(2,128)(2,1)S(1)}, u32[]{:S(2)}, u32[]{:S(2)}) collective-permute-start(bf16[128,2,128]{2,1,0:T(2,128)(2,1)} %param.4), channel_id=1, source_target_pairs={{0,24},{8,16},{16,8},{24,0},{1,25},{9,17},{17,9},{25,1},{2,26},{10... | collective-permute-start | bytes 196616 | tf_op jit(solution)/shard_map/ppermute | solution.py:237
  0.8 2.6 %collective-permute-start.1 = (bf16[256,128]{1,0:T(8,128)(2,1)}, bf16[256,128]{1,0:T(8,128)(2,1)S(1)}, u32[]{:S(2)}, u32[]{:S(2)}) collective-permute-start(bf16[256,128]{1,0:T(8,128)(2,1)} %bitcast.7), channel_id=1, source_target_pairs={{0,8},{8,0},{16,24},{24,16},{1,9},{9,1},{17,25},{25,17},{2,10},{10... | collective-permute-start | bytes 196616 | tf_op jit(solution)/shard_map/ppermute | solution.py:250
  0.8 2.6 %collective-permute-start.2 = (bf16[128,2,128]{2,1,0:T(2,128)(2,1)}, bf16[128,2,128]{2,1,0:T(2,128)(2,1)S(1)}, u32[]{:S(2)}, u32[]{:S(2)}) collective-permute-start(bf16[128,2,128]{2,1,0:T(2,128)(2,1)} %param.5), channel_id=1, source_target_pairs={{0,8},{8,0},{16,24},{24,16},{1,9},{9,1},{17,25},{25,17},{2,10},{10... | collective-permute-start | bytes 196616 | tf_op jit(solution)/shard_map/ppermute | solution.py:249
  1.3 2.1 %copy-start = (bf16[128,32,128]{2,1,0:T(8,128)(2,1)S(1)}, bf16[128,32,128]{2,1,0:T(8,128)(2,1)}, u32[]{:S(2)}) copy-start(bf16[128,32,128]{2,1,0:T(8,128)(2,1)} %refs_0_.3) | copy-start | bytes 3145732
  1.3 5.0 %collective-permute-start.4 = (bf16[256,128]{1,0:T(8,128)(2,1)}, bf16[256,128]{1,0:T(8,128)(2,1)S(1)}, u32[]{:S(2)}, u32[]{:S(2)}) collective-permute-start(bf16[256,128]{1,0:T(8,128)(2,1)} %bitcast.9), channel_id=1, source_target_pairs={{0,24},{8,16},{16,8},{24,0},{1,25},{9,17},{17,9},{25,1},{2,26},{10... | collective-permute-start | bytes 196616 | tf_op jit(solution)/shard_map/ppermute | solution.py:237
  4.9 1.5 %collective-permute-start.3 = (bf16[256,128]{1,0:T(8,128)(2,1)S(1)}, bf16[256,128]{1,0:T(8,128)(2,1)S(1)}, u32[]{:S(2)}, u32[]{:S(2)}) collective-permute-start(bf16[256,128]{1,0:T(8,128)(2,1)S(1)} %bitcast.4), channel_id=1, source_target_pairs={{0,8},{8,0},{16,24},{24,16},{1,9},{9,1},{17,25},{25,17},{2,10},{10... | collective-permute-start | bytes 196616 | tf_op jit(solution)/shard_map/ppermute | solution.py:308
  6.4 1.5 %collective-permute-start.5 = (bf16[256,128]{1,0:T(8,128)(2,1)S(1)}, bf16[256,128]{1,0:T(8,128)(2,1)S(1)}, u32[]{:S(2)}, u32[]{:S(2)}) collective-permute-start(bf16[256,128]{1,0:T(8,128)(2,1)S(1)} %collective-permute-done.4.refs_0_), channel_id=1, source_target_pairs={{0,8},{8,0},{16,24},{24,16},{1,9},{9,1},{17,25},{25,17},{2,10},{10... | collective-permute-start | bytes 196616 | tf_op jit(solution)/shard_map/ppermute | solution.py:311

commit v4 on v3

--- a/solution.py
+++ b/solution.py
@@ -28,6 +28,19 @@
     for head in range(kv_heads):
         block = wide_ref[pl.ds(head, count, stride=kv_heads), :]
         block_ref[head, base : base + count, :depth] = block.astype(packed.dtype)
+
+
+def split_keys(packed, kv_heads, factor, base, wide_ref, keys_ref):
+    total, depth = packed.shape
+    count = total // kv_heads
+    wide_ref[...] = packed.astype(jnp.float32) * factor
+    for head in range(kv_heads):
+        block = wide_ref[pl.ds(head, count, stride=kv_heads), :]
+        high = block.astype(packed.dtype)
+        keys_ref[head, base : base + count, :depth] = high
+        keys_ref[head, base : base + count, depth:] = (
+            block - high.astype(jnp.float32)
+        ).astype(packed.dtype)
 
 
 def fill_ones(values_ref, depth):
@@ -108,7 +121,7 @@
                 scores = own
             top = jnp.max(scores, axis=1, keepdims=True)
             weights = jnp.exp2((scores - top) * factor).astype(values_ref.dtype)
-            top_ref[head, where, :] = jnp.broadcast_to(top, (tile_rows, depth))
+            top_ref[head, where, :] = jnp.broadcast_to(top * factor, (tile_rows, depth))
             sums_ref[head, where, :] = jnp.dot(
                 weights, values_ref[head], preferred_element_type=jnp.float32
             )
@@ -132,20 +145,22 @@
     @pl.when(chip >= hop)
     def _():
         for block in range(pair):
-            split_into(key_refs[block][...], kv_heads, block * rows, wide_ref.at[block], keys_ref)
+            split_keys(
+                key_refs[block][...], kv_heads, factor, block * rows, wide_ref.at[block], keys_ref
+            )
         for tile in range(tiles):
             where = slice(tile * tile_rows, (tile + 1) * tile_rows)
             for head in range(kv_heads):
                 q_rows = tile_queries(q_ref, head, group, tile, positions)
-                scores = scores_of(q_rows, keys_ref[head])
+                scores = scores_of(jnp.concatenate([q_rows, q_rows], axis=1), keys_ref[head])
                 old = old_ref[head, where, :]
                 top = jnp.maximum(jnp.max(scores, axis=1, keepdims=True), old)
                 if top_ref is not None:
                     top_ref[head, where, :] = top
-                drop_ref[head, where, :] = (old - top) * factor
+                drop_ref[head, where, :] = old - top
                 for part in range(pair * rows // depth):
                     weights_ref[head, part, where, :] = jnp.exp2(
-                        (scores[:, part * depth : (part + 1) * depth] - top) * factor
+                        scores[:, part * depth : (part + 1) * depth] - top
                     ).astype(weights_ref.dtype)
 
     @pl.when(chip == hop - 1)
@@ -259,6 +274,7 @@
         return pltpu.VMEM((count, *keys.shape), jnp.float32)
 
     keys_scratch = pltpu.VMEM((kv_heads, pair * rows, depth), keys.dtype)
+    parts_scratch = pltpu.VMEM((kv_heads, pair * rows, 2 * depth), keys.dtype)
     values_scratch = pltpu.VMEM((kv_heads, pair * rows, 2 * depth), keys.dtype)
     out_scratch = [pltpu.VMEM(queries.shape, queries.dtype), pltpu.SemaphoreType.DMA((tiles,))]
     params = pltpu.CompilerParams(vmem_limit_bytes=VMEM_LIMIT)
@@ -315,7 +331,7 @@
             out_shape=(weights_shape, top_shape, out_shape) + (() if last else (top_shape,)),
             in_specs=[vmem] * (3 + pair) + [anywhere] * len(held),
             out_specs=(vmem, vmem, anywhere) + (() if last else (vmem,)),
-            scratch_shapes=[wide_scratch(pair), keys_scratch, *out_scratch],
+            scratch_shapes=[wide_scratch(pair), parts_scratch, *out_scratch],
             input_output_aliases={3 + pair: 2} if held else {},
             compiler_params=params,
             cost_estimate=cost,

time: 9.59 us -> 9.47 us (0.987)
  Pallas kernels: 5.11 us -> 5.01 us
    pallas_call x1, Pallas kernels: 1.13 us -> 1.02 us  [local(): pl.pallas_call(functools.partial(keys_kernel, 'ctx', pair, kv_heads, fact...]
  transfers between devices with their start and end apart: 6 -> 6, of which waited for: 2 -> 2; matrix products, arithmetic and copies ran while one was open for 0% -> 0% of each run, Pallas kernels for 38% -> 37%
where the time goes in v4:
time: 9.47 us; the launch traced here: 9.33 us
  Pallas kernels  5.01 us (53%)
  starting transfers between devices  3.33 us (35%)
  waiting for transfers between devices  0.93 us (10%)
    ppermute x2, starting transfers between devices, across(): return lax.ppermute(array, 'ctx', route).reshape(rows * kv_heads, depth)  1.91 us
    pallas_call x1, Pallas kernels, local(): pl.pallas_call(functools.partial(values_kernel, 'ctx', pair, kv_heads, ho...  1.58 us
    pallas_call x1, Pallas kernels, local(): pl.pallas_call(functools.partial(first_kernel, 'ctx', pair, kv_heads, fac...  1.49 us
    pallas_call x1, Pallas kernels, local(): pl.pallas_call(functools.partial(keys_kernel, 'ctx', pair, kv_heads, fact...  1.02 us
    pallas_call x1, Pallas kernels, local(): pl.pallas_call(functools.partial(load_kernel, kv_heads), out_shape=(pltpu...  0.91 us
    ppermute x2, waiting for transfers between devices, across(): return lax.ppermute(array, 'ctx', route).reshape(rows * kv_heads, depth)  0.84 us
    ppermute x1, starting transfers between devices, local(): all_keys.append(lax.ppermute(first_keys, 'ctx', swap))  0.56 us
    ppermute x1, starting transfers between devices, local(): lax.ppermute(raw_values, 'ctx', swap).reshape(rows * kv_heads, depth)  0.51 us
  transfers between devices with their start and end apart: 6, of which 2 were waited for; matrix products, arithmetic and copies ran while one was open for 0% of the time, Pallas kernels for 37%

profile of v4, /device:TPU:7, one launch (start us, length us, event | category | flops | bytes accessed | tf_op | source)
XLA Modules:
  0.0 9.3 jit_solution(16026675813429036906)
XLA Ops:
  0.0 0.8 %collective-permute-start = (bf16[128,2,128]{2,1,0:T(2,128)(2,1)}, bf16[128,2,128]{2,1,0:T(2,128)(2,1)S(1)}, u32[]{:S(2)}, u32[]{:S(2)}) collective-permute-start(bf16[128,2,128]{2,1,0:T(2,128)(2,1)} %param.4), channel_id=1, source_target_pairs={{0,24},{8,16},{16,8},{24,0},{1,25},{9,17},{17,9},{25,1},{2,26},{10... | collective-permute-start | bytes 196616 | tf_op jit(solution)/shard_map/ppermute | solution.py:252
  0.8 0.0 collective-permute-start.1
  0.8 0.5 %collective-permute-start.2 = (bf16[128,2,128]{2,1,0:T(2,128)(2,1)}, bf16[128,2,128]{2,1,0:T(2,128)(2,1)S(1)}, u32[]{:S(2)}, u32[]{:S(2)}) collective-permute-start(bf16[128,2,128]{2,1,0:T(2,128)(2,1)} %param.5), channel_id=1, source_target_pairs={{0,8},{8,0},{16,24},{24,16},{1,9},{9,1},{17,25},{25,17},{2,10},{10... | collective-permute-start | bytes 196616 | tf_op jit(solution)/shard_map/ppermute | solution.py:264
  1.3 0.0 copy-start
  1.3 1.1 %collective-permute-start.4 = (bf16[256,128]{1,0:T(8,128)(2,1)}, bf16[256,128]{1,0:T(8,128)(2,1)S(1)}, u32[]{:S(2)}, u32[]{:S(2)}) collective-permute-start(bf16[256,128]{1,0:T(8,128)(2,1)} %bitcast.9), channel_id=1, source_target_pairs={{0,24},{8,16},{16,8},{24,0},{1,25},{9,17},{17,9},{25,1},{2,26},{10... | collective-permute-start | bytes 196616 | tf_op jit(solution)/shard_map/ppermute | solution.py:252
  2.4 0.9 %shard_map.37 = (bf16[2,128,128]{2,1,0:T(8,128)(2,1)S(1)}, bf16[2,128,256]{2,1,0:T(8,128)(2,1)S(1)}) custom-call(bf16[256,128]{1,0:T(8,128)(2,1)} %bitcast.8, bf16[256,128]{1,0:T(8,128)(2,1)} %bitcast.10), custom_call_target="tpu_custom_call" | custom-call | flops 53687091200 | bytes 104857600 | tf_op jit(solution)/shard_map/pallas_call | solution.py:288
  3.4 0.0 collective-permute-done.1.refs_3_
  3.4 0.0 collective-permute-done.2
  3.4 0.0 copy-done
  3.4 1.5 %shard_map.38 = (f32[2,2048,128]{2,1,0:T(8,128)S(1)}, f32[2,2048,256]{2,1,0:T(8,128)S(1)}) custom-call(bf16[128,32,128]{2,1,0:T(8,128)(2,1)S(1)} %copy-done, bf16[2,128,128]{2,1,0:T(8,128)(2,1)S(1)} %get-tuple-element.17.refs_1_, bf16[2,128,256]{2,1,0:T(8,128)(2,1)S(1)} %get-tuple-element.18.refs_2_, bf16[256,128]{1,0:T(8,128)(2,1)S(1)} %collective-permute-done.1.refs_3_, ...), custom_call_target="tpu_custom_call" | custom-call | flops 53687091200 | bytes 104857600 | tf_op jit(solution)/shard_map/pallas_call | solution.py:305
  4.9 0.0 collective-permute-done
  4.9 0.6 %collective-permute-start.3 = (bf16[256,128]{1,0:T(8,128)(2,1)S(1)}, bf16[256,128]{1,0:T(8,128)(2,1)S(1)}, u32[]{:S(2)}, u32[]{:S(2)}) collective-permute-start(bf16[256,128]{1,0:T(8,128)(2,1)S(1)} %bitcast.4), channel_id=1, source_target_pairs={{0,8},{8,0},{16,24},{24,16},{1,9},{9,1},{17,25},{25,17},{2,10},{10... | collective-permute-start | bytes 196616 | tf_op jit(solution)/shard_map/ppermute | solution.py:324
  5.5 0.8 %collective-permute-done.4.refs_0_ = bf16[256,128]{1,0:T(8,128)(2,1)S(1)} collective-permute-done((bf16[256,128]{1,0:T(8,128)(2,1)}, bf16[256,128]{1,0:T(8,128)(2,1)S(1)}, u32[]{:S(2)}, u32[]{:S(2)}) %collective-permute-start.4) | collective-permute-done | bytes 65568 | tf_op jit(solution)/shard_map/ppermute | solution.py:252
  6.3 0.1 collective-permute-done.3.refs_2_
  6.4 0.4 %collective-permute-start.5 = (bf16[256,128]{1,0:T(8,128)(2,1)S(1)}, bf16[256,128]{1,0:T(8,128)(2,1)S(1)}, u32[]{:S(2)}, u32[]{:S(2)}) collective-permute-start(bf16[256,128]{1,0:T(8,128)(2,1)S(1)} %collective-permute-done.4.refs_0_), channel_id=1, source_target_pairs={{0,8},{8,0},{16,24},{24,16},{1,9},{9,1},{17,25},{25,17},{2,10},{10... | collective-permute-start | bytes 196616 | tf_op jit(solution)/shard_map/ppermute | solution.py:327
  6.7 1.0 %shard_map.39 = (bf16[2,2,2048,128]{3,2,1,0:T(8,128)(2,1)S(1)}, f32[2,2048,128]{2,1,0:T(8,128)S(1)}, bf16[128,32,128]{2,1,0:T(8,128)(2,1)}) custom-call(bf16[128,32,128]{2,1,0:T(8,128)(2,1)S(1)} %copy-done, bf16[256,128]{1,0:T(8,128)(2,1)S(1)} %bitcast.5, bf16[256,128]{1,0:T(8,128)(2,1)S(1)} %collective-permute-done.3.refs_2_, ...), custom_call_target="tpu_custom_call" | custom-call | flops 536870912 | bytes 1048576 | tf_op jit(solution)/shard_map/pallas_call | solution.py:329
  7.7 0.0 collective-permute-done.5.refs_1_
  7.7 1.6 %shard_map.40 = (f32[2,2048,256]{2,1,0:T(8,128)S(1)}, bf16[128,32,128]{2,1,0:T(8,128)(2,1)}) custom-call(bf16[256,128]{1,0:T(8,128)(2,1)S(1)} %collective-permute-done.4.refs_0_, bf16[256,128]{1,0:T(8,128)(2,1)S(1)} %collective-permute-done.5.refs_1_, ...), custom_call_target="tpu_custom_call", output_to_operand_aliasing={{0}: (4, {}), {1}: (5, {})} | custom-call | flops 536870912 | bytes 1048576 | tf_op jit(solution)/shard_map/pallas_call | solution.py:346
Async XLA Ops:
  0.0 4.9 %collective-permute-start = (bf16[128,2,128]{2,1,0:T(2,128)(2,1)}, bf16[128,2,128]{2,1,0:T(2,128)(2,1)S(1)}, u32[]{:S(2)}, u32[]{:S(2)}) collective-permute-start(bf16[128,2,128]{2,1,0:T(2,128)(2,1)} %param.4), channel_id=1, source_target_pairs={{0,24},{8,16},{16,8},{24,0},{1,25},{9,17},{17,9},{25,1},{2,26},{10... | collective-permute-start | bytes 196616 | tf_op jit(solution)/shard_map/ppermute | solution.py:252
  0.8 2.6 %collective-permute-start.1 = (bf16[256,128]{1,0:T(8,128)(2,1)}, bf16[256,128]{1,0:T(8,128)(2,1)S(1)}, u32[]{:S(2)}, u32[]{:S(2)}) collective-permute-start(bf16[256,128]{1,0:T(8,128)(2,1)} %bitcast.7), channel_id=1, source_target_pairs={{0,8},{8,0},{16,24},{24,16},{1,9},{9,1},{17,25},{25,17},{2,10},{10... | collective-permute-start | bytes 196616 | tf_op jit(solution)/shard_map/ppermute | solution.py:265
  0.8 2.6 %collective-permute-start.2 = (bf16[128,2,128]{2,1,0:T(2,128)(2,1)}, bf16[128,2,128]{2,1,0:T(2,128)(2,1)S(1)}, u32[]{:S(2)}, u32[]{:S(2)}) collective-permute-start(bf16[128,2,128]{2,1,0:T(2,128)(2,1)} %param.5), channel_id=1, source_target_pairs={{0,8},{8,0},{16,24},{24,16},{1,9},{9,1},{17,25},{25,17},{2,10},{10... | collective-permute-start | bytes 196616 | tf_op jit(solution)/shard_map/ppermute | solution.py:264
  1.3 2.1 %copy-start = (bf16[128,32,128]{2,1,0:T(8,128)(2,1)S(1)}, bf16[128,32,128]{2,1,0:T(8,128)(2,1)}, u32[]{:S(2)}) copy-start(bf16[128,32,128]{2,1,0:T(8,128)(2,1)} %refs_0_.3) | copy-start | bytes 3145732
  1.3 5.0 %collective-permute-start.4 = (bf16[256,128]{1,0:T(8,128)(2,1)}, bf16[256,128]{1,0:T(8,128)(2,1)S(1)}, u32[]{:S(2)}, u32[]{:S(2)}) collective-permute-start(bf16[256,128]{1,0:T(8,128)(2,1)} %bitcast.9), channel_id=1, source_target_pairs={{0,24},{8,16},{16,8},{24,0},{1,25},{9,17},{17,9},{25,1},{2,26},{10... | collective-permute-start | bytes 196616 | tf_op jit(solution)/shard_map/ppermute | solution.py:252
  4.9 1.5 %collective-permute-start.3 = (bf16[256,128]{1,0:T(8,128)(2,1)S(1)}, bf16[256,128]{1,0:T(8,128)(2,1)S(1)}, u32[]{:S(2)}, u32[]{:S(2)}) collective-permute-start(bf16[256,128]{1,0:T(8,128)(2,1)S(1)} %bitcast.4), channel_id=1, source_target_pairs={{0,8},{8,0},{16,24},{24,16},{1,9},{9,1},{17,25},{25,17},{2,10},{10... | collective-permute-start | bytes 196616 | tf_op jit(solution)/shard_map/ppermute | solution.py:324
  6.4 1.4 %collective-permute-start.5 = (bf16[256,128]{1,0:T(8,128)(2,1)S(1)}, bf16[256,128]{1,0:T(8,128)(2,1)S(1)}, u32[]{:S(2)}, u32[]{:S(2)}) collective-permute-start(bf16[256,128]{1,0:T(8,128)(2,1)S(1)} %collective-permute-done.4.refs_0_), channel_id=1, source_target_pairs={{0,8},{8,0},{16,24},{24,16},{1,9},{9,1},{17,25},{25,17},{2,10},{10... | collective-permute-start | bytes 196616 | tf_op jit(solution)/shard_map/ppermute | solution.py:327

commit v5 on v4

--- a/solution.py
+++ b/solution.py
@@ -11,7 +11,6 @@
 VMEM_LIMIT = 30 * 1024 * 1024
 TILE_ROWS = 512
 NEG = -1e30
-DIRECT = False
 
 
 def tile_plan(rows, group):
@@ -127,14 +126,34 @@
             )
 
 
+def write_kernel(axis, pair, kv_heads, hop, *refs):
+    sums_ref, out_ref, stage_ref, out_sems = refs[0], *refs[-3:]
+    rows, heads, depth = stage_ref.shape
+    group = heads // kv_heads
+    positions = tile_plan(rows, group)
+    tile_rows = positions * group
+    tiles = rows // positions
+
+    @pl.when(lax.div(lax.axis_index(axis), pair) == hop - 1)
+    def _():
+        for tile in range(tiles):
+            where = slice(tile * tile_rows, (tile + 1) * tile_rows)
+            for head in range(kv_heads):
+                put_result(
+                    stage_ref, head, group, tile, positions,
+                    sums_ref[head, where, :depth], sums_ref[head, where, depth:],
+                )
+            out_copy(stage_ref, out_ref, out_sems, tile, positions).start()
+        for tile in range(tiles):
+            out_copy(stage_ref, out_ref, out_sems, tile, positions).wait()
+
+
 def keys_kernel(axis, pair, kv_heads, factor, hop, last, *refs):
     q_ref = refs[0]
     key_refs = refs[1 : 1 + pair]
-    old_ref, sums_ref = refs[1 + pair : 3 + pair]
-    held = hop > 1
-    weights_ref, drop_ref, out_ref = refs[3 + held + pair : 6 + held + pair]
-    top_ref = None if last else refs[6 + held + pair]
-    wide_ref, keys_ref, stage_ref, out_sems = refs[-4:]
+    old_ref, weights_ref, drop_ref = refs[1 + pair : 4 + pair]
+    top_ref = None if last else refs[4 + pair]
+    wide_ref, keys_ref = refs[-2:]
     rows, heads, depth = q_ref.shape
     group = heads // kv_heads
     positions = tile_plan(rows, group)
@@ -163,19 +182,6 @@
                         scores[:, part * depth : (part + 1) * depth] - top
                     ).astype(weights_ref.dtype)
 
-    @pl.when(chip == hop - 1)
-    def _():
-        for tile in range(tiles):
-            where = slice(tile * tile_rows, (tile + 1) * tile_rows)
-            for head in range(kv_heads):
-                put_result(
-                    stage_ref, head, group, tile, positions,
-                    sums_ref[head, where, :depth], sums_ref[head, where, depth:],
-                )
-            out_copy(stage_ref, out_ref, out_sems, tile, positions).start()
-        for tile in range(tiles):
-            out_copy(stage_ref, out_ref, out_sems, tile, positions).wait()
-
 
 def values_kernel(axis, pair, kv_heads, hop, last, *refs):
     value_refs = refs[:pair]
@@ -254,8 +260,6 @@
     def far_pair(hop):
         far_keys = [across(raw_keys, hop, pair - 1)]
         far_values = [across(values, hop, pair - 1)]
-        if pair == 2 and DIRECT:
-            far_values.append(across(values, hop, 0))
         return far_keys, far_values
 
     far = [far_pair(1)]
@@ -270,6 +274,7 @@
     cost = pl.CostEstimate(
         flops=work * depth * 4, bytes_accessed=heads * rows * depth * 2, transcendentals=work
     )
+
     def wide_scratch(count):
         return pltpu.VMEM((count, *keys.shape), jnp.float32)
 
@@ -318,30 +323,32 @@
         if not last:
             far.append(far_pair(hop + 1))
         all_keys, all_values = far[hop - 1]
-        first_keys, top = lax.optimization_barrier((all_keys[0], top))
+        held = [] if out is None else [in_hbm(out)]
+        out = pl.pallas_call(
+            functools.partial(write_kernel, "ctx", pair, kv_heads, hop),
+            out_shape=out_shape,
+            in_specs=[vmem] + [anywhere] * len(held),
+            out_specs=anywhere,
+            scratch_shapes=out_scratch,
+            input_output_aliases={1: 0} if held else {},
+            compiler_params=params,
+            cost_estimate=cost,
+        )(in_vmem(sums), *held)
+        first_keys, top, out = lax.optimization_barrier((all_keys[0], top, out))
         all_keys = [first_keys]
         if pair == 2:
             all_keys.append(lax.ppermute(first_keys, "ctx", swap))
-            if not DIRECT:
-                all_keys[1], first_values = lax.optimization_barrier((all_keys[1], all_values[0]))
-                all_values = [first_values, lax.ppermute(first_values, "ctx", swap)]
-        held = [] if out is None else [in_hbm(out)]
-        weights, drop, out, *new_top = pl.pallas_call(
+            first_values, sums = lax.optimization_barrier((all_values[0], sums))
+            all_values = [first_values, lax.ppermute(first_values, "ctx", swap)]
+        weights, drop, *new_top = pl.pallas_call(
             functools.partial(keys_kernel, "ctx", pair, kv_heads, factor, hop, last),
-            out_shape=(weights_shape, top_shape, out_shape) + (() if last else (top_shape,)),
-            in_specs=[vmem] * (3 + pair) + [anywhere] * len(held),
-            out_specs=(vmem, vmem, anywhere) + (() if last else (vmem,)),
-            scratch_shapes=[wide_scratch(pair), parts_scratch, *out_scratch],
-            input_output_aliases={3 + pair: 2} if held else {},
+            out_shape=(weights_shape, top_shape) + (() if last else (top_shape,)),
+            in_specs=[vmem] * (2 + pair),
+            out_specs=(vmem, vmem) + (() if last else (vmem,)),
+            scratch_shapes=[wide_scratch(pair), parts_scratch],
             compiler_params=params,
             cost_estimate=cost,
-        )(
-            in_vmem(q_vmem),
-            *[in_vmem(x) for x in all_keys],
-            in_vmem(top),
-            in_vmem(sums),
-            *held,
-        )
+        )(*[in_vmem(x) for x in (q_vmem, *all_keys, top)])
         top = top if last else new_top[0]
         sums, out = pl.pallas_call(
             functools.partial(values_kernel, "ctx", pair, kv_heads, hop, last),

time: 9.47 us -> 9.4 us (level)
  waiting for transfers between devices: 0.93 us -> 0.77 us
  transfers between devices with their start and end apart: 6 -> 6, of which waited for: 2 -> 1; matrix products, arithmetic and copies ran while one was open for 0% -> 0% of each run, Pallas kernels for 37% -> 37%
where the time goes in v5:
time: 9.4 us; the launch traced here: 9.25 us
  Pallas kernels  5.02 us (53%)
  starting transfers between devices  3.39 us (36%)
  waiting for transfers between devices  0.77 us (8%)
    ppermute x2, starting transfers between devices, across(): return lax.ppermute(array, 'ctx', route).reshape(rows * kv_heads, depth)  1.91 us
    pallas_call x1, Pallas kernels, local(): pl.pallas_call(functools.partial(values_kernel, 'ctx', pair, kv_heads, ho...  1.58 us
    pallas_call x1, Pallas kernels, local(): pl.pallas_call(functools.partial(first_kernel, 'ctx', pair, kv_heads, fac...  1.49 us
    pallas_call x1, Pallas kernels, local(): pl.pallas_call(functools.partial(keys_kernel, 'ctx', pair, kv_heads, fact...  0.98 us
    pallas_call x1, Pallas kernels, local(): pl.pallas_call(functools.partial(load_kernel, kv_heads), out_shape=(pltpu...  0.91 us
    ppermute x2, waiting for transfers between devices, across(): return lax.ppermute(array, 'ctx', route).reshape(rows * kv_heads, depth)  0.76 us
    ppermute x1, starting transfers between devices, local(): all_keys.append(lax.ppermute(first_keys, 'ctx', swap))  0.57 us
    ppermute x1, starting transfers between devices, local(): lax.ppermute(raw_values, 'ctx', swap).reshape(rows * kv_heads, depth)  0.51 us
  transfers between devices with their start and end apart: 6, of which 1 were waited for; matrix products, arithmetic and copies ran while one was open for 0% of the time, Pallas kernels for 37%

profile of v5, /device:TPU:7, one launch (start us, length us, event | category | flops | bytes accessed | tf_op | source)
XLA Modules:
  0.0 9.3 jit_solution(3109336303841724857)
XLA Ops:
  0.0 0.8 %collective-permute-start.4 = (bf16[128,2,128]{2,1,0:T(2,128)(2,1)}, bf16[128,2,128]{2,1,0:T(2,128)(2,1)S(1)}, u32[]{:S(2)}, u32[]{:S(2)}) collective-permute-start(bf16[128,2,128]{2,1,0:T(2,128)(2,1)} %param.4), channel_id=1, source_target_pairs={{0,24},{8,16},{16,8},{24,0},{1,25},{9,17},{17,9},{25,1},{2,26},{10... | collective-permute-start | bytes 196616 | tf_op jit(solution)/shard_map/ppermute | solution.py:258
  0.8 0.0 collective-permute-start.1
  0.8 0.5 %collective-permute-start.2 = (bf16[128,2,128]{2,1,0:T(2,128)(2,1)}, bf16[128,2,128]{2,1,0:T(2,128)(2,1)S(1)}, u32[]{:S(2)}, u32[]{:S(2)}) collective-permute-start(bf16[128,2,128]{2,1,0:T(2,128)(2,1)} %param.5), channel_id=1, source_target_pairs={{0,8},{8,0},{16,24},{24,16},{1,9},{9,1},{17,25},{25,17},{2,10},{10... | collective-permute-start | bytes 196616 | tf_op jit(solution)/shard_map/ppermute | solution.py:268
  1.3 0.0 copy-start
  1.3 1.1 %collective-permute-start = (bf16[256,128]{1,0:T(8,128)(2,1)}, bf16[256,128]{1,0:T(8,128)(2,1)S(1)}, u32[]{:S(2)}, u32[]{:S(2)}) collective-permute-start(bf16[256,128]{1,0:T(8,128)(2,1)} %bitcast.9), channel_id=1, source_target_pairs={{0,24},{8,16},{16,8},{24,0},{1,25},{9,17},{17,9},{25,1},{2,26},{10... | collective-permute-start | bytes 196616 | tf_op jit(solution)/shard_map/ppermute | solution.py:258
  2.4 0.9 %shard_map.37 = (bf16[2,128,128]{2,1,0:T(8,128)(2,1)S(1)}, bf16[2,128,256]{2,1,0:T(8,128)(2,1)S(1)}) custom-call(bf16[256,128]{1,0:T(8,128)(2,1)} %bitcast.8, bf16[256,128]{1,0:T(8,128)(2,1)} %bitcast.10), custom_call_target="tpu_custom_call" | custom-call | flops 53687091200 | bytes 104857600 | tf_op jit(solution)/shard_map/pallas_call | solution.py:293
  3.4 0.0 collective-permute-done.1.refs_3_
  3.4 0.0 collective-permute-done.2
  3.4 0.0 copy-done
  3.4 1.5 %shard_map.38 = (f32[2,2048,128]{2,1,0:T(8,128)S(1)}, f32[2,2048,256]{2,1,0:T(8,128)S(1)}) custom-call(bf16[128,32,128]{2,1,0:T(8,128)(2,1)S(1)} %copy-done, bf16[2,128,128]{2,1,0:T(8,128)(2,1)S(1)} %get-tuple-element.17.refs_1_, bf16[2,128,256]{2,1,0:T(8,128)(2,1)S(1)} %get-tuple-element.18.refs_2_, bf16[256,128]{1,0:T(8,128)(2,1)S(1)} %collective-permute-done.1.refs_3_, ...), custom_call_target="tpu_custom_call" | custom-call | flops 53687091200 | bytes 104857600 | tf_op jit(solution)/shard_map/pallas_call | solution.py:310
  4.9 0.1 shard_map.39.refs_5_
  4.9 0.0 collective-permute-done.4
  4.9 0.6 %collective-permute-start.5 = (bf16[256,128]{1,0:T(8,128)(2,1)S(1)}, bf16[256,128]{1,0:T(8,128)(2,1)S(1)}, u32[]{:S(2)}, u32[]{:S(2)}) collective-permute-start(bf16[256,128]{1,0:T(8,128)(2,1)S(1)} %bitcast.4), channel_id=1, source_target_pairs={{0,8},{8,0},{16,24},{24,16},{1,9},{9,1},{17,25},{25,17},{2,10},{10... | collective-permute-start | bytes 196616 | tf_op jit(solution)/shard_map/ppermute | solution.py:340
  5.5 0.8 %collective-permute-done.refs_0_ = bf16[256,128]{1,0:T(8,128)(2,1)S(1)} collective-permute-done((bf16[256,128]{1,0:T(8,128)(2,1)}, bf16[256,128]{1,0:T(8,128)(2,1)S(1)}, u32[]{:S(2)}, u32[]{:S(2)}) %collective-permute-start) | collective-permute-done | bytes 65568 | tf_op jit(solution)/shard_map/ppermute | solution.py:258
  6.3 0.4 %collective-permute-start.3 = (bf16[256,128]{1,0:T(8,128)(2,1)S(1)}, bf16[256,128]{1,0:T(8,128)(2,1)S(1)}, u32[]{:S(2)}, u32[]{:S(2)}) collective-permute-start(bf16[256,128]{1,0:T(8,128)(2,1)S(1)} %collective-permute-done.refs_0_), channel_id=1, source_target_pairs={{0,8},{8,0},{16,24},{24,16},{1,9},{9,1},{17,25},{25,17},{2,10},{10... | collective-permute-start | bytes 196616 | tf_op jit(solution)/shard_map/ppermute | solution.py:342
  6.7 0.0 collective-permute-done.5.refs_2_
  6.7 1.0 %shard_map.40 = (bf16[2,2,2048,128]{3,2,1,0:T(8,128)(2,1)S(1)}, f32[2,2048,128]{2,1,0:T(8,128)S(1)}) custom-call(bf16[128,32,128]{2,1,0:T(8,128)(2,1)S(1)} %copy-done, bf16[256,128]{1,0:T(8,128)(2,1)S(1)} %bitcast.5, bf16[256,128]{1,0:T(8,128)(2,1)S(1)} %collective-permute-done.5.refs_2_, f32[2,2048,128]{2,1,0:T(8,128)S(1)} %get-tuple-element.23.refs_3_), custom_call_target="tpu_custom_call" | custom-call | flops 536870912 | bytes 1048576 | tf_op jit(solution)/shard_map/pallas_call | solution.py:343
  7.7 0.0 collective-permute-done.3.refs_1_
  7.7 1.6 %shard_map.41 = (f32[2,2048,256]{2,1,0:T(8,128)S(1)}, bf16[128,32,128]{2,1,0:T(8,128)(2,1)}) custom-call(bf16[256,128]{1,0:T(8,128)(2,1)S(1)} %collective-permute-done.refs_0_, bf16[256,128]{1,0:T(8,128)(2,1)S(1)} %collective-permute-done.3.refs_1_, ...), custom_call_target="tpu_custom_call", output_to_operand_aliasing={{0}: (4, {}), {1}: (5, {})} | custom-call | flops 536870912 | bytes 1048576 | tf_op jit(solution)/shard_map/pallas_call | solution.py:353
Async XLA Ops:
  0.0 4.9 %collective-permute-start.4 = (bf16[128,2,128]{2,1,0:T(2,128)(2,1)}, bf16[128,2,128]{2,1,0:T(2,128)(2,1)S(1)}, u32[]{:S(2)}, u32[]{:S(2)}) collective-permute-start(bf16[128,2,128]{2,1,0:T(2,128)(2,1)} %param.4), channel_id=1, source_target_pairs={{0,24},{8,16},{16,8},{24,0},{1,25},{9,17},{17,9},{25,1},{2,26},{10... | collective-permute-start | bytes 196616 | tf_op jit(solution)/shard_map/ppermute | solution.py:258
  0.8 2.6 %collective-permute-start.1 = (bf16[256,128]{1,0:T(8,128)(2,1)}, bf16[256,128]{1,0:T(8,128)(2,1)S(1)}, u32[]{:S(2)}, u32[]{:S(2)}) collective-permute-start(bf16[256,128]{1,0:T(8,128)(2,1)} %bitcast.7), channel_id=1, source_target_pairs={{0,8},{8,0},{16,24},{24,16},{1,9},{9,1},{17,25},{25,17},{2,10},{10... | collective-permute-start | bytes 196616 | tf_op jit(solution)/shard_map/ppermute | solution.py:269
  0.8 2.6 %collective-permute-start.2 = (bf16[128,2,128]{2,1,0:T(2,128)(2,1)}, bf16[128,2,128]{2,1,0:T(2,128)(2,1)S(1)}, u32[]{:S(2)}, u32[]{:S(2)}) collective-permute-start(bf16[128,2,128]{2,1,0:T(2,128)(2,1)} %param.5), channel_id=1, source_target_pairs={{0,8},{8,0},{16,24},{24,16},{1,9},{9,1},{17,25},{25,17},{2,10},{10... | collective-permute-start | bytes 196616 | tf_op jit(solution)/shard_map/ppermute | solution.py:268
  1.3 2.1 %copy-start = (bf16[128,32,128]{2,1,0:T(8,128)(2,1)S(1)}, bf16[128,32,128]{2,1,0:T(8,128)(2,1)}, u32[]{:S(2)}) copy-start(bf16[128,32,128]{2,1,0:T(8,128)(2,1)} %refs_0_.3) | copy-start | bytes 3145732
  1.3 5.0 %collective-permute-start = (bf16[256,128]{1,0:T(8,128)(2,1)}, bf16[256,128]{1,0:T(8,128)(2,1)S(1)}, u32[]{:S(2)}, u32[]{:S(2)}) collective-permute-start(bf16[256,128]{1,0:T(8,128)(2,1)} %bitcast.9), channel_id=1, source_target_pairs={{0,24},{8,16},{16,8},{24,0},{1,25},{9,17},{17,9},{25,1},{2,26},{10... | collective-permute-start | bytes 196616 | tf_op jit(solution)/shard_map/ppermute | solution.py:258
  4.9 1.7 %collective-permute-start.5 = (bf16[256,128]{1,0:T(8,128)(2,1)S(1)}, bf16[256,128]{1,0:T(8,128)(2,1)S(1)}, u32[]{:S(2)}, u32[]{:S(2)}) collective-permute-start(bf16[256,128]{1,0:T(8,128)(2,1)S(1)} %bitcast.4), channel_id=1, source_target_pairs={{0,8},{8,0},{16,24},{24,16},{1,9},{9,1},{17,25},{25,17},{2,10},{10... | collective-permute-start | bytes 196616 | tf_op jit(solution)/shard_map/ppermute | solution.py:340
  6.3 1.4 %collective-permute-start.3 = (bf16[256,128]{1,0:T(8,128)(2,1)S(1)}, bf16[256,128]{1,0:T(8,128)(2,1)S(1)}, u32[]{:S(2)}, u32[]{:S(2)}) collective-permute-start(bf16[256,128]{1,0:T(8,128)(2,1)S(1)} %collective-permute-done.refs_0_), channel_id=1, source_target_pairs={{0,8},{8,0},{16,24},{24,16},{1,9},{9,1},{17,25},{25,17},{2,10},{10... | collective-permute-start | bytes 196616 | tf_op jit(solution)/shard_map/ppermute | solution.py:342

commit v6 on v5

--- a/solution.py
+++ b/solution.py
@@ -148,39 +148,66 @@
             out_copy(stage_ref, out_ref, out_sems, tile, positions).wait()
 
 
-def keys_kernel(axis, pair, kv_heads, factor, hop, last, *refs):
-    q_ref = refs[0]
-    key_refs = refs[1 : 1 + pair]
-    old_ref, weights_ref, drop_ref = refs[1 + pair : 4 + pair]
-    top_ref = None if last else refs[4 + pair]
-    wide_ref, keys_ref = refs[-2:]
+def early_kernel(axis, pair, kv_heads, factor, hop, *refs):
+    q_ref, key_ref, old_ref, scores_ref, top_ref, wide_ref, keys_ref = refs
     rows, heads, depth = q_ref.shape
     group = heads // kv_heads
     positions = tile_plan(rows, group)
     tile_rows = positions * group
     tiles = rows // positions
-    chip = lax.div(lax.axis_index(axis), pair)
-
-    @pl.when(chip >= hop)
+
+    @pl.when(lax.div(lax.axis_index(axis), pair) >= hop)
     def _():
-        for block in range(pair):
-            split_keys(
-                key_refs[block][...], kv_heads, factor, block * rows, wide_ref.at[block], keys_ref
-            )
+        split_keys(key_ref[...], kv_heads, factor, 0, wide_ref.at[0], keys_ref)
         for tile in range(tiles):
             where = slice(tile * tile_rows, (tile + 1) * tile_rows)
             for head in range(kv_heads):
                 q_rows = tile_queries(q_ref, head, group, tile, positions)
                 scores = scores_of(jnp.concatenate([q_rows, q_rows], axis=1), keys_ref[head])
-                old = old_ref[head, where, :]
-                top = jnp.maximum(jnp.max(scores, axis=1, keepdims=True), old)
+                scores_ref[head, where, :] = scores
+                top_ref[head, where, :] = jnp.maximum(
+                    jnp.max(scores, axis=1, keepdims=True), old_ref[head, where, :]
+                )
+
+
+def keys_kernel(axis, pair, kv_heads, factor, hop, last, *refs):
+    q_ref, old_ref, early_ref, early_top_ref = refs[:4]
+    key_refs = refs[4 : 3 + pair]
+    weights_ref, drop_ref = refs[3 + pair : 5 + pair]
+    top_ref = None if last else refs[5 + pair]
+    wide_ref, keys_ref = refs[-2:]
+    rows, heads, depth = q_ref.shape
+    group = heads // kv_heads
+    positions = tile_plan(rows, group)
+    tile_rows = positions * group
+    tiles = rows // positions
+    chip = lax.div(lax.axis_index(axis), pair)
+
+    @pl.when(chip >= hop)
+    def _():
+        for at, key_ref in enumerate(key_refs):
+            split_keys(key_ref[...], kv_heads, factor, at * rows, wide_ref.at[at], keys_ref)
+        for tile in range(tiles):
+            where = slice(tile * tile_rows, (tile + 1) * tile_rows)
+            for head in range(kv_heads):
+                scores = [early_ref[head, where, :]]
+                top = early_top_ref[head, where, :]
+                if key_refs:
+                    q_rows = tile_queries(q_ref, head, group, tile, positions)
+                    scores.append(
+                        scores_of(jnp.concatenate([q_rows, q_rows], axis=1), keys_ref[head])
+                    )
+                    top = jnp.maximum(jnp.max(scores[1], axis=1, keepdims=True), top)
                 if top_ref is not None:
                     top_ref[head, where, :] = top
-                drop_ref[head, where, :] = old - top
-                for part in range(pair * rows // depth):
-                    weights_ref[head, part, where, :] = jnp.exp2(
-                        scores[:, part * depth : (part + 1) * depth] - top
-                    ).astype(weights_ref.dtype)
+                drop_ref[head, where, :] = old_ref[head, where, :] - top
+                part = 0
+                for piece in scores:
+                    for at in range(0, piece.shape[1], depth):
+                        weights_ref[head, part, where, :] = jnp.exp2(
+                            piece[:, at : at + depth] - top
+                        ).astype(weights_ref.dtype)
+                        part += 1
 
 
 def values_kernel(axis, pair, kv_heads, hop, last, *refs):
@@ -279,7 +306,8 @@
         return pltpu.VMEM((count, *keys.shape), jnp.float32)
 
     keys_scratch = pltpu.VMEM((kv_heads, pair * rows, depth), keys.dtype)
-    parts_scratch = pltpu.VMEM((kv_heads, pair * rows, 2 * depth), keys.dtype)
+    early_scratch = pltpu.VMEM((kv_heads, rows, 2 * depth), keys.dtype)
+    early_shape = pltpu.VMEM((kv_heads, rows * group, rows), jnp.float32)
     values_scratch = pltpu.VMEM((kv_heads, pair * rows, 2 * depth), keys.dtype)
     out_scratch = [pltpu.VMEM(queries.shape, queries.dtype), pltpu.SemaphoreType.DMA((tiles,))]
     params = pltpu.CompilerParams(vmem_limit_bytes=VMEM_LIMIT)
@@ -336,19 +364,28 @@
         )(in_vmem(sums), *held)
         first_keys, top, out = lax.optimization_barrier((all_keys[0], top, out))
         all_keys = [first_keys]
+        early, early_top = pl.pallas_call(
+            functools.partial(early_kernel, "ctx", pair, kv_heads, factor, hop),
+            out_shape=(early_shape, top_shape),
+            in_specs=[vmem] * 3,
+            out_specs=(vmem,) * 2,
+            scratch_shapes=[wide_scratch(1), early_scratch],
+            compiler_params=params,
+            cost_estimate=cost,
+        )(*[in_vmem(x) for x in (q_vmem, all_keys[0], top)])
         if pair == 2:
             all_keys.append(lax.ppermute(first_keys, "ctx", swap))
-            first_values, sums = lax.optimization_barrier((all_values[0], sums))
+            first_values, early_top = lax.optimization_barrier((all_values[0], early_top))
             all_values = [first_values, lax.ppermute(first_values, "ctx", swap)]
         weights, drop, *new_top = pl.pallas_call(
             functools.partial(keys_kernel, "ctx", pair, kv_heads, factor, hop, last),
             out_shape=(weights_shape, top_shape) + (() if last else (top_shape,)),
-            in_specs=[vmem] * (2 + pair),
+            in_specs=[vmem] * (3 + pair),
             out_specs=(vmem, vmem) + (() if last else (vmem,)),
-            scratch_shapes=[wide_scratch(pair), parts_scratch],
+            scratch_shapes=[wide_scratch(1), early_scratch],
             compiler_params=params,
             cost_estimate=cost,
-        )(*[in_vmem(x) for x in (q_vmem, *all_keys, top)])
+        )(*[in_vmem(x) for x in (q_vmem, top, early, early_top, *all_keys[1:])])
         top = top if last else new_top[0]
         sums, out = pl.pallas_call(
             functools.partial(values_kernel, "ctx", pair, kv_heads, hop, last),

time: 9.4 us -> 9.37 us (level)
  Pallas kernels: 5.02 us -> 5.76 us
  waiting for transfers between devices: 0.77 us -> 0.07 us
    pallas_call x0 -> x1, Pallas kernels: none -> 0.81 us  [local(): pl.pallas_call(functools.partial(early_kernel, 'ctx', pair, kv_heads, fac...]
    ppermute x2, waiting for transfers between devices: 0.76 us -> 0.01 us  [across(): return lax.ppermute(array, 'ctx', route).reshape(rows * kv_heads, depth)]
  transfers between devices with their start and end apart: 6 -> 6, of which waited for: 1 -> 1; matrix products, arithmetic and copies ran while one was open for 0% -> 0% of each run, Pallas kernels for 37% -> 46%
where the time goes in v6:
time: 9.37 us; the launch traced here: 9.23 us
  Pallas kernels  5.76 us (61%)
  starting transfers between devices  3.32 us (35%)
    ppermute x2, starting transfers between devices, across(): return lax.ppermute(array, 'ctx', route).reshape(rows * kv_heads, depth)  1.91 us
    pallas_call x1, Pallas kernels, local(): pl.pallas_call(functools.partial(values_kernel, 'ctx', pair, kv_heads, ho...  1.56 us
    pallas_call x1, Pallas kernels, local(): pl.pallas_call(functools.partial(first_kernel, 'ctx', pair, kv_heads, fac...  1.49 us
    pallas_call x1, Pallas kernels, local(): pl.pallas_call(functools.partial(keys_kernel, 'ctx', pair, kv_heads, fact...  0.93 us
    pallas_call x1, Pallas kernels, local(): pl.pallas_call(functools.partial(load_kernel, kv_heads), out_shape=(pltpu...  0.91 us
    pallas_call x1, Pallas kernels, local(): pl.pallas_call(functools.partial(early_kernel, 'ctx', pair, kv_heads, fac...  0.81 us
    ppermute x1, starting transfers between devices, local(): all_keys.append(lax.ppermute(first_keys, 'ctx', swap))  0.57 us
    ppermute x1, starting transfers between devices, local(): lax.ppermute(raw_values, 'ctx', swap).reshape(rows * kv_heads, depth)  0.51 us
  transfers between devices with their start and end apart: 6, of which 1 were waited for; matrix products, arithmetic and copies ran while one was open for 0% of the time, Pallas kernels for 46%

profile of v6, /device:TPU:7, one launch (start us, length us, event | category | flops | bytes accessed | tf_op | source)
XLA Modules:
  0.0 9.2 jit_solution(9309552409978681843)
XLA Ops:
  0.0 0.8 %collective-permute-start.1 = (bf16[128,2,128]{2,1,0:T(2,128)(2,1)}, bf16[128,2,128]{2,1,0:T(2,128)(2,1)S(1)}, u32[]{:S(2)}, u32[]{:S(2)}) collective-permute-start(bf16[128,2,128]{2,1,0:T(2,128)(2,1)} %param.4), channel_id=1, source_target_pairs={{0,24},{8,16},{16,8},{24,0},{1,25},{9,17},{17,9},{25,1},{2,26},{10... | collective-permute-start | bytes 196616 | tf_op jit(solution)/shard_map/ppermute | solution.py:285
  0.8 0.0 collective-permute-start.2
  0.8 0.5 %collective-permute-start.3 = (bf16[128,2,128]{2,1,0:T(2,128)(2,1)}, bf16[128,2,128]{2,1,0:T(2,128)(2,1)S(1)}, u32[]{:S(2)}, u32[]{:S(2)}) collective-permute-start(bf16[128,2,128]{2,1,0:T(2,128)(2,1)} %param.5), channel_id=1, source_target_pairs={{0,8},{8,0},{16,24},{24,16},{1,9},{9,1},{17,25},{25,17},{2,10},{10... | collective-permute-start | bytes 196616 | tf_op jit(solution)/shard_map/ppermute | solution.py:295
  1.3 0.0 copy-start
  1.3 1.1 %collective-permute-start = (bf16[256,128]{1,0:T(8,128)(2,1)}, bf16[256,128]{1,0:T(8,128)(2,1)S(1)}, u32[]{:S(2)}, u32[]{:S(2)}) collective-permute-start(bf16[256,128]{1,0:T(8,128)(2,1)} %bitcast.9), channel_id=1, source_target_pairs={{0,24},{8,16},{16,8},{24,0},{1,25},{9,17},{17,9},{25,1},{2,26},{10... | collective-permute-start | bytes 196616 | tf_op jit(solution)/shard_map/ppermute | solution.py:285
  2.4 0.9 %shard_map.37 = (bf16[2,128,128]{2,1,0:T(8,128)(2,1)S(1)}, bf16[2,128,256]{2,1,0:T(8,128)(2,1)S(1)}) custom-call(bf16[256,128]{1,0:T(8,128)(2,1)} %bitcast.8, bf16[256,128]{1,0:T(8,128)(2,1)} %bitcast.10), custom_call_target="tpu_custom_call" | custom-call | flops 53687091200 | bytes 104857600 | tf_op jit(solution)/shard_map/pallas_call | solution.py:321
  3.4 0.0 collective-permute-done.2.refs_3_
  3.4 0.0 collective-permute-done.3
  3.4 0.0 copy-done
  3.4 1.5 %shard_map.38 = (f32[2,2048,128]{2,1,0:T(8,128)S(1)}, f32[2,2048,256]{2,1,0:T(8,128)S(1)}) custom-call(bf16[128,32,128]{2,1,0:T(8,128)(2,1)S(1)} %copy-done, bf16[2,128,128]{2,1,0:T(8,128)(2,1)S(1)} %get-tuple-element.19.refs_1_, bf16[2,128,256]{2,1,0:T(8,128)(2,1)S(1)} %get-tuple-element.20.refs_2_, bf16[256,128]{1,0:T(8,128)(2,1)S(1)} %collective-permute-done.2.refs_3_, ...), custom_call_target="tpu_custom_call" | custom-call | flops 53687091200 | bytes 104857600 | tf_op jit(solution)/shard_map/pallas_call | solution.py:338
  4.9 0.1 shard_map.39.refs_5_
  4.9 0.0 collective-permute-done.1
  4.9 0.6 %collective-permute-start.5 = (bf16[256,128]{1,0:T(8,128)(2,1)S(1)}, bf16[256,128]{1,0:T(8,128)(2,1)S(1)}, u32[]{:S(2)}, u32[]{:S(2)}) collective-permute-start(bf16[256,128]{1,0:T(8,128)(2,1)S(1)} %bitcast.4), channel_id=1, source_target_pairs={{0,8},{8,0},{16,24},{24,16},{1,9},{9,1},{17,25},{25,17},{2,10},{10... | collective-permute-start | bytes 196616 | tf_op jit(solution)/shard_map/ppermute | solution.py:377
  5.5 0.8 %shard_map.40 = (f32[2,2048,128]{2,1,0:T(8,128)S(1)}, f32[2,2048,128]{2,1,0:T(8,128)S(1)}) custom-call(bf16[128,32,128]{2,1,0:T(8,128)(2,1)S(1)} %copy-done, bf16[256,128]{1,0:T(8,128)(2,1)S(1)} %bitcast.5, f32[2,2048,128]{2,1,0:T(8,128)S(1)} %get-tuple-element.24.refs_2_.refs_1_), custom_call_target="tpu_custom_call" | custom-call | flops 536870912 | bytes 1048576 | tf_op jit(solution)/shard_map/pallas_call | solution.py:367
  6.3 0.0 collective-permute-done.refs_0_
  6.3 0.3 %collective-permute-start.4 = (bf16[256,128]{1,0:T(8,128)(2,1)S(1)}, bf16[256,128]{1,0:T(8,128)(2,1)S(1)}, u32[]{:S(2)}, u32[]{:S(2)}) collective-permute-start(bf16[256,128]{1,0:T(8,128)(2,1)S(1)} %collective-permute-done.refs_0_), channel_id=1, source_target_pairs={{0,8},{8,0},{16,24},{24,16},{1,9},{9,1},{17,25},{25,17},{2,10},{10... | collective-permute-start | bytes 196616 | tf_op jit(solution)/shard_map/ppermute | solution.py:379
  6.7 0.0 collective-permute-done.5.refs_4_
  6.7 0.9 %shard_map.41 = (bf16[2,2,2048,128]{3,2,1,0:T(8,128)(2,1)S(1)}, f32[2,2048,128]{2,1,0:T(8,128)S(1)}) custom-call(bf16[128,32,128]{2,1,0:T(8,128)(2,1)S(1)} %copy-done, f32[2,2048,128]{2,1,0:T(8,128)S(1)} %get-tuple-element.24.refs_2_.refs_1_, f32[2,2048,128]{2,1,0:T(8,128)S(1)} %get-tuple-element.27.refs_2_, f32[2,2048,128]{2,1,0:T(8,128)S(1)} %get-tuple-element.28.refs_3_, ...), custom_call_target="tpu_custom_call" | custom-call | flops 536870912 | bytes 1048576 | tf_op jit(solution)/shard_map/pallas_call | solution.py:380
  7.6 0.1 collective-permute-done.4.refs_1_
  7.7 1.6 %shard_map.42 = (f32[2,2048,256]{2,1,0:T(8,128)S(1)}, bf16[128,32,128]{2,1,0:T(8,128)(2,1)}) custom-call(bf16[256,128]{1,0:T(8,128)(2,1)S(1)} %collective-permute-done.refs_0_, bf16[256,128]{1,0:T(8,128)(2,1)S(1)} %collective-permute-done.4.refs_1_, ...), custom_call_target="tpu_custom_call", output_to_operand_aliasing={{0}: (4, {}), {1}: (5, {})} | custom-call | flops 536870912 | bytes 1048576 | tf_op jit(solution)/shard_map/pallas_call | solution.py:390
Async XLA Ops:
  0.0 4.9 %collective-permute-start.1 = (bf16[128,2,128]{2,1,0:T(2,128)(2,1)}, bf16[128,2,128]{2,1,0:T(2,128)(2,1)S(1)}, u32[]{:S(2)}, u32[]{:S(2)}) collective-permute-start(bf16[128,2,128]{2,1,0:T(2,128)(2,1)} %param.4), channel_id=1, source_target_pairs={{0,24},{8,16},{16,8},{24,0},{1,25},{9,17},{17,9},{25,1},{2,26},{10... | collective-permute-start | bytes 196616 | tf_op jit(solution)/shard_map/ppermute | solution.py:285
  0.8 2.6 %collective-permute-start.2 = (bf16[256,128]{1,0:T(8,128)(2,1)}, bf16[256,128]{1,0:T(8,128)(2,1)S(1)}, u32[]{:S(2)}, u32[]{:S(2)}) collective-permute-start(bf16[256,128]{1,0:T(8,128)(2,1)} %bitcast.7), channel_id=1, source_target_pairs={{0,8},{8,0},{16,24},{24,16},{1,9},{9,1},{17,25},{25,17},{2,10},{10... | collective-permute-start | bytes 196616 | tf_op jit(solution)/shard_map/ppermute | solution.py:296
  0.8 2.6 %collective-permute-start.3 = (bf16[128,2,128]{2,1,0:T(2,128)(2,1)}, bf16[128,2,128]{2,1,0:T(2,128)(2,1)S(1)}, u32[]{:S(2)}, u32[]{:S(2)}) collective-permute-start(bf16[128,2,128]{2,1,0:T(2,128)(2,1)} %param.5), channel_id=1, source_target_pairs={{0,8},{8,0},{16,24},{24,16},{1,9},{9,1},{17,25},{25,17},{2,10},{10... | collective-permute-start | bytes 196616 | tf_op jit(solution)/shard_map/ppermute | solution.py:295
  1.3 2.1 %copy-start = (bf16[128,32,128]{2,1,0:T(8,128)(2,1)S(1)}, bf16[128,32,128]{2,1,0:T(8,128)(2,1)}, u32[]{:S(2)}) copy-start(bf16[128,32,128]{2,1,0:T(8,128)(2,1)} %refs_0_.5) | copy-start | bytes 3145732
  1.3 5.0 %collective-permute-start = (bf16[256,128]{1,0:T(8,128)(2,1)}, bf16[256,128]{1,0:T(8,128)(2,1)S(1)}, u32[]{:S(2)}, u32[]{:S(2)}) collective-permute-start(bf16[256,128]{1,0:T(8,128)(2,1)} %bitcast.9), channel_id=1, source_target_pairs={{0,24},{8,16},{16,8},{24,0},{1,25},{9,17},{17,9},{25,1},{2,26},{10... | collective-permute-start | bytes 196616 | tf_op jit(solution)/shard_map/ppermute | solution.py:285
  4.9 1.7 %collective-permute-start.5 = (bf16[256,128]{1,0:T(8,128)(2,1)S(1)}, bf16[256,128]{1,0:T(8,128)(2,1)S(1)}, u32[]{:S(2)}, u32[]{:S(2)}) collective-permute-start(bf16[256,128]{1,0:T(8,128)(2,1)S(1)} %bitcast.4), channel_id=1, source_target_pairs={{0,8},{8,0},{16,24},{24,16},{1,9},{9,1},{17,25},{25,17},{2,10},{10... | collective-permute-start | bytes 196616 | tf_op jit(solution)/shard_map/ppermute | solution.py:377
  6.3 1.3 %collective-permute-start.4 = (bf16[256,128]{1,0:T(8,128)(2,1)S(1)}, bf16[256,128]{1,0:T(8,128)(2,1)S(1)}, u32[]{:S(2)}, u32[]{:S(2)}) collective-permute-start(bf16[256,128]{1,0:T(8,128)(2,1)S(1)} %collective-permute-done.refs_0_), channel_id=1, source_target_pairs={{0,8},{8,0},{16,24},{24,16},{1,9},{9,1},{17,25},{25,17},{2,10},{10... | collective-permute-start | bytes 196616 | tf_op jit(solution)/shard_map/ppermute | solution.py:379
